TPU v7x, 128 devices: a whole 4x4x4 slice. The times are simulated.
128 devices in a mesh: front: 32 (over z, y, core), blk: 4 (over x).
Axes of the slice: x: 4, y: 4, z: 4, core: 2. Of those that a mesh axis runs over, the one named last changes fastest.
Arguments:
- root_tiles: bfloat16 [32, 5, 640, 10240], P('front', None, None, 'blk'), as said below
- child_tiles: bfloat16 [32, 3, 256, 4096], P('front', None, None, 'blk'), as said below
- child_update: bfloat16 [49152, 2, 4096], P('front', None, 'blk'), may hold values from -0.0625 to 0.0625
- extend_map: int32 [384], P('front'), may hold values from 0 to 319, as said below
- root_side: float32 [32, 2, 24, 640], P('front'), may hold values from -6 to 6
- child_side: float32 [32, 2, 24, 256], P('front'), may hold values from -6 to 6
Outputs:
- root_field: float32 [32, 2, 24, 640], P('front')
- child_field: float32 [32, 2, 24, 256], P('front')
Inputs may be any that keep to these rules, and one draw needn't show every extreme that they name: `extend_map`: within one child the 192 blocks name distinct root blocks. Root block r lies in panel k = r div (80) and stripe q = (r mod (80)) div (5) and is held by front index 16 * min(k, 3 - k) + q. The 12 entries held by one front index name at most 1 root blocks held by any one front index, and exactly 1 for some. `root_tiles`: diagonal slots are upper triangular with diagonal entries between 0.75 and 1.25. `child_tiles`: diagonal slots are upper triangular with diagonal entries between 0.75 and 1.25.
All inputs are finite; a program needn't handle non-finite values.
Results may differ from a plain program's by a relative error of at most 0.0003.
Values sent between devices are 32-bit elements; how exact they have to be, the bound alone decides.
A program may use at most 128 MiB of HBM per device.

v0:
```python
import jax
import jax.numpy as jnp
from jax import lax
from jax.sharding import PartitionSpec as P

BLOCK_ROWS = 128


exact_mode = lax.Precision.HIGHEST


def times_tile(vector, tile):
    return jnp.dot(vector, tile.astype(jnp.float32), precision=exact_mode)


def times_tile_transposed(vector, tile):
    return lax.dot_general(
        vector, tile.astype(jnp.float32), (((1,), (1,)), ((), ())), precision=exact_mode
    )


def across_blk(partial_rows):
    pieces = lax.all_gather(partial_rows, "blk", axis=0, tiled=True)
    return jnp.sum(pieces.reshape((lax.axis_size("blk"),) + partial_rows.shape), axis=0)


def across_front(stacked):
    return lax.psum(stacked, "front")


def panel_place(step_index, panels):
    lower = jnp.minimum(step_index, panels - 1 - step_index)
    second = (step_index != lower).astype(jnp.int32)
    return (lower, second)


def own_slot(which, pair_index, panels, column):
    if which == 0:
        mine = pair_index
        slot_index = column
    else:
        mine = panels - 1 - pair_index
        slot_index = pair_index + 1 + column
    return (mine, jnp.clip(slot_index, 0, panels))


def forward_chain(factor_tiles, right_side, running, groups, member, pair_index):
    panels = factor_tiles.shape[0] - 1
    leading = lax.axis_index("blk") == 0
    solved = jnp.zeros((panels, right_side.shape[1], factor_tiles.shape[2]), jnp.float32)

    def advance(step_index, state):
        running, solved = state
        lower, second = panel_place(step_index, panels)
        owner = pair_index == lower
        partial_rows = jnp.where(leading, right_side[second], 0.0) - running[second]
        whole_rows = across_blk(partial_rows)
        diag_slot = jnp.where(second == 1, panels, lower)
        term = jnp.where(owner, times_tile(whole_rows, factor_tiles[diag_slot]), 0.0)
        stacked = jnp.zeros((groups,) + term.shape, jnp.float32).at[member].set(term)
        piece = across_front(stacked)[member]
        solved = solved.at[step_index].set(piece)
        for which in range(2):
            mine, slot_index = own_slot(which, pair_index, panels, step_index)
            update = lax.cond(
                step_index < mine,
                lambda: times_tile_transposed(piece, factor_tiles[slot_index]),
                lambda: jnp.zeros(running.shape[1:], jnp.float32),
            )
            running = running.at[which].add(update)
        return (running, solved)

    return lax.fori_loop(0, panels, advance, (running, solved))[1]


def push_rows(incoming, whole_rows, lower, second, factor_tiles, panels):

    def spread(slot_index, incoming):
        valid = jnp.where(
            second == 0, slot_index < lower, (slot_index > lower) & (slot_index < panels)
        )
        target = jnp.clip(jnp.where(second == 0, slot_index, slot_index - lower - 1), 0, panels - 1)
        addend = times_tile(whole_rows, factor_tiles[slot_index])
        return incoming.at[target].add(jnp.where(valid, addend, 0.0))

    return lax.fori_loop(0, panels + 1, spread, incoming)


def backward_chain(factor_tiles, solved, incoming, groups, member, pair_index):
    panels = factor_tiles.shape[0] - 1
    directions = solved.shape[1]
    finished = jnp.zeros((2, directions, factor_tiles.shape[1]), jnp.float32)

    def retreat(count_index, state):
        incoming, finished = state
        step_index = panels - 1 - count_index
        lower, second = panel_place(step_index, panels)
        owner = pair_index == lower
        collected = incoming[step_index]
        stacked = jnp.zeros((groups,) + collected.shape, jnp.float32).at[member].set(collected)
        total = across_front(stacked)[member]
        rest = solved[step_index] - total
        diag_slot = jnp.where(second == 1, panels, lower)
        term = times_tile_transposed(rest, factor_tiles[diag_slot])
        whole_rows = across_blk(term)
        finished = jnp.where(owner, finished.at[second].set(whole_rows), finished)
        incoming = lax.cond(
            owner,
            lambda: push_rows(incoming, whole_rows, lower, second, factor_tiles, panels),
            lambda: incoming,
        )
        return (incoming, finished)

    return lax.fori_loop(0, panels, retreat, (incoming, finished))[1]


def child_products(solved, update_rows):

    def add_panel(panel_index, total):
        slab = lax.dynamic_index_in_dim(update_rows, panel_index, 1, keepdims=False)
        return total + times_tile_transposed(solved[panel_index], slab)

    start = jnp.zeros((solved.shape[1], update_rows.shape[0]), jnp.float32)
    return lax.fori_loop(0, solved.shape[0], add_panel, start)


def child_transposed(needed, update_rows):
    panels = update_rows.shape[1]

    def one_panel(panel_index, result):
        slab = lax.dynamic_index_in_dim(update_rows, panel_index, 1, keepdims=False)
        return result.at[panel_index].set(times_tile(needed, slab))

    start = jnp.zeros((panels, needed.shape[0], update_rows.shape[2]), jnp.float32)
    return lax.fori_loop(0, panels, one_panel, start)


def route_plan(extend_map, root_panels, stripe_blocks, split, fronts, capacity):
    panel_blocks = split * stripe_blocks
    column_index = extend_map // panel_blocks
    within_panel = extend_map % panel_blocks
    stripe_index = within_panel // stripe_blocks
    within_block = within_panel % stripe_blocks
    lower = jnp.minimum(column_index, root_panels - 1 - column_index)
    second = (column_index != lower).astype(jnp.int32)
    owner_device = split * lower + stripe_index
    owner_slot = second * stripe_blocks + within_block
    positions = jnp.arange(extend_map.shape[0])
    earlier = (owner_device[:, None] == owner_device[None, :]) & (
        positions[None, :] < positions[:, None]
    )
    ranking = jnp.sum(earlier.astype(jnp.int32), axis=1)
    target = owner_device * capacity + ranking
    matches = jnp.arange(fronts * capacity)[:, None] == target[None, :]
    choose = matches.astype(jnp.float32)
    slot_tags = jnp.max(jnp.where(matches, owner_slot[None, :], -1), axis=1)
    return (choose, slot_tags)


def on_device(root_tiles, child_tiles, child_update, extend_map, root_side, child_side):
    fronts = lax.axis_size("front")
    position = lax.axis_index("front")
    half_count = fronts // 2
    split = fronts // 2
    member = position // half_count
    child_pair = position % half_count // split
    root_pair = position // split
    root_local = root_tiles[0]
    child_local = child_tiles[0]
    root_rhs = root_side[0]
    child_rhs = child_side[0]
    directions = child_rhs.shape[1]
    child_solved = forward_chain(
        child_local, child_rhs, jnp.zeros_like(child_rhs), 2, member, child_pair
    )
    products = child_products(child_solved, child_update)
    root_panels = root_local.shape[0] - 1
    stripe_rows = root_local.shape[1]
    stripe_blocks = stripe_rows // BLOCK_ROWS
    slot_count = extend_map.shape[0]
    capacity = (slot_count + fronts - 1) // fronts
    choose, slot_tags = route_plan(extend_map, root_panels, stripe_blocks, split, fronts, capacity)
    sent_rows = products.shape[0]
    blocks = products.reshape(sent_rows, slot_count, BLOCK_ROWS)
    outgoing = jnp.einsum("us,dsk->udk", choose, blocks, precision=exact_mode)
    outgoing = outgoing.reshape(fronts, capacity, sent_rows, BLOCK_ROWS)
    arrived, arrived_tags = (
        lax.all_to_all(outgoing, "front", split_axis=0, concat_axis=0, tiled=True),
        lax.all_to_all(
            slot_tags.reshape(fronts, capacity), "front", split_axis=0, concat_axis=0, tiled=True
        ),
    )
    placing = (jnp.arange(2 * stripe_blocks)[:, None] == arrived_tags.reshape(-1)[None, :]).astype(
        jnp.float32
    )
    landed = jnp.einsum(
        "su,udk->sdk",
        placing,
        arrived.reshape(fronts * capacity, sent_rows, BLOCK_ROWS),
        precision=exact_mode,
    )
    landed = (
        landed.reshape(2, stripe_blocks, sent_rows, BLOCK_ROWS)
        .transpose(0, 2, 1, 3)
        .reshape(2, sent_rows, stripe_rows)
    )
    root_solved = forward_chain(root_local, root_rhs, landed, 1, 0, root_pair)
    root_field = backward_chain(
        root_local, root_solved, jnp.zeros_like(root_solved), 1, 0, root_pair
    )
    root_blocks = root_field.reshape(2, directions, stripe_blocks, BLOCK_ROWS).transpose(0, 2, 1, 3)
    root_blocks = root_blocks.reshape(2 * stripe_blocks, directions, BLOCK_ROWS)
    returning = jnp.einsum("su,sdk->udk", placing, root_blocks, precision=exact_mode)
    returning = returning.reshape(fronts, capacity, directions, BLOCK_ROWS)
    answered = lax.all_to_all(returning, "front", split_axis=0, concat_axis=0, tiled=True)
    needed = jnp.einsum(
        "us,udk->dsk",
        choose,
        answered.reshape(fronts * capacity, directions, BLOCK_ROWS),
        precision=exact_mode,
    )
    needed = needed.reshape(directions, slot_count * BLOCK_ROWS)
    child_incoming = child_transposed(needed, child_update)
    child_field = backward_chain(child_local, child_solved, child_incoming, 2, member, child_pair)
    return (root_field[None], child_field[None])


def solution(mesh):
    in_specs = (
        P("front", None, None, "blk"),
        P("front", None, None, "blk"),
        P("front", None, "blk"),
        P("front"),
        P("front", None, None, None),
        P("front", None, None, None),
    )
    out_specs = (P("front", None, None, None), P("front", None, None, None))
    return jax.shard_map(
        on_device, mesh=mesh, in_specs=in_specs, out_specs=out_specs, check_vma=False
    )
```

profile of v0, /device:TPU:1, one launch (start us, length us, event | category | flops | bytes accessed | tf_op | source)
XLA Modules:
  0.0 1645.5 jit_solution(17929524444404206275)
XLA Ops:
  9.5 9.6 all-to-all-start
  19.2 7.5 copy.28
  26.9 231.0 %while.148 = (s32[]{:T(128)}, f32[2,24,256]{2,1,0:T(8,128)S(1)}, f32[2,24,1024]{2,1,0:T(8,128)S(1)}, s32[]{:T(128)}, s32[3]{0:T(128)S(1)}, /*index=5*/pred[3]{0:...) while((s32[]{:T(128)}, f32[2,24,256]{2,1,0:T(8,128)S(1)}, ...), condition=%wide.region_11.12_spmd, body=%wide.region_2.11_spmd.sunk | while | flops 226658336 | bytes 4964975 | solution.py:73
  27.0 9.8 all-gather.4
  39.9 101.3 %all-reduce.5.cloned.1.call-done = f32[2,24,1024]{2,1,0:T(8,128)} async-done(((f32[2,24,1024]{2,1,0:T(8,128)}), f32[2,24,1024]{2,1,0:T(8,128)}) %all-reduce.5.cloned.1.call-update) | async-done | bytes 196624 | tf_op jit(solution)/shard_map/while/body/eval_jaxpr/psum | solution.py:28
  143.5 9.3 all-gather.4
  155.9 100.3 %all-reduce.5.cloned.1.call-done = f32[2,24,1024]{2,1,0:T(8,128)} async-done(((f32[2,24,1024]{2,1,0:T(8,128)}), f32[2,24,1024]{2,1,0:T(8,128)}) %all-reduce.5.cloned.1.call-update) | async-done | bytes 196624 | tf_op jit(solution)/shard_map/while/body/eval_jaxpr/psum | solution.py:28
  257.9 8.9 while.153
  257.9 4.4 fusion.166
  262.4 4.4 fusion.166
  268.4 5.9 all-to-all-start.1
  275.0 9.5 all-to-all-done.1
  284.9 489.5 %while.149 = (s32[]{:T(128)}, f32[2,24,640]{2,1,0:T(8,128)S(1)}, f32[4,24,2560]{2,1,0:T(8,128)S(1)}, s32[]{:T(128)}, pred[]{:T(512)}, /*index=5*/f32[2,24,640]{2...) while((s32[]{:T(128)}, f32[2,24,640]{2,1,0:T(8,128)S(1)}, ...), condition=%wide.region_22.23_spmd, body=%wide.region_14.22_spmd.sunk | while | flops 1415869440 | bytes 14131758 | solution.py:73
  285.0 10.2 all-gather.5
  295.2 4.0 fusion.151
  300.0 99.9 %all-reduce.7.cloned.1.call-done = f32[1,24,2560]{2,1,0:T(8,128)} async-done(((f32[1,24,2560]{2,1,0:T(8,128)}), f32[1,24,2560]{2,1,0:T(8,128)}) %all-reduce.7.cloned.1.call-update) | async-done | bytes 245776 | tf_op jit(solution)/shard_map/while/body/eval_jaxpr/psum | solution.py:28
  399.9 4.6 conditional.15
  399.9 4.6 fusion.23
  406.3 10.2 all-gather.5
  416.5 4.0 fusion.151
  421.3 106.0 %all-reduce.7.cloned.1.call-done = f32[1,24,2560]{2,1,0:T(8,128)} async-done(((f32[1,24,2560]{2,1,0:T(8,128)}), f32[1,24,2560]{2,1,0:T(8,128)}) %all-reduce.7.cloned.1.call-update) | async-done | bytes 245776 | tf_op jit(solution)/shard_map/while/body/eval_jaxpr/psum | solution.py:28
  527.3 4.6 conditional.15
  527.3 4.6 fusion.23
  533.7 10.2 all-gather.5
  543.8 4.0 fusion.151
  548.7 101.5 %all-reduce.7.cloned.1.call-done = f32[1,24,2560]{2,1,0:T(8,128)} async-done(((f32[1,24,2560]{2,1,0:T(8,128)}), f32[1,24,2560]{2,1,0:T(8,128)}) %all-reduce.7.cloned.1.call-update) | async-done | bytes 245776 | tf_op jit(solution)/shard_map/while/body/eval_jaxpr/psum | solution.py:28
  650.1 4.6 conditional.15
  650.2 4.6 fusion.23
  656.5 10.2 all-gather.5
  666.7 4.0 fusion.151
  671.5 101.2 %all-reduce.7.cloned.1.call-done = f32[1,24,2560]{2,1,0:T(8,128)} async-done(((f32[1,24,2560]{2,1,0:T(8,128)}), f32[1,24,2560]{2,1,0:T(8,128)}) %all-reduce.7.cloned.1.call-update) | async-done | bytes 245776 | tf_op jit(solution)/shard_map/while/body/eval_jaxpr/psum | solution.py:28
  775.5 590.8 %while.150 = (s32[]{:T(128)}, f32[4,24,2560]{2,1,0:T(8,128)S(1)}, f32[2,24,640]{2,1,0:T(8,128)S(1)}, s32[]{:T(128)}, f32[4,24,2560]{2,1,0:T(8,128)}, /*index=5*/...) while((s32[]{:T(128)}, f32[4,24,2560]{2,1,0:T(8,128)S(1)}, ...), condition=%wide.region_32.33_spmd, body=%wide.region_23.32_spmd.sunk | while | flops 944102400 | bytes 10426675 | solution.py:114
  777.1 103.6 %all-reduce.9.cloned.1.call-done = f32[1,24,2560]{2,1,0:T(8,128)} async-done(((f32[1,24,2560]{2,1,0:T(8,128)}), f32[1,24,2560]{2,1,0:T(8,128)}) %all-reduce.9.cloned.1.call-update) | async-done | bytes 245776 | tf_op jit(solution)/shard_map/while/body/eval_jaxpr/psum | solution.py:28
  880.7 4.8 fusion.155
  885.5 10.2 all_gather.44
  895.7 26.2 %conditional.16 = (f32[4,24,2560]{2,1,0:T(8,128)S(1)}) conditional(s32[]{:T(128)} %convert_element_type.157, f32[4,24,2560]{2,1,0:T(8,128)S(1)} %get-tuple-element.2510, (s32[]{:T(128)}, s32[]{:T(128)}, bf16[5,640,2560]{2,1,0:T(8,128)(2,1)}, f32[24,640]{1,0:T(8,128)S(1)}, f32[4,24,2560]{2,1,0:T(8,128)S(1)}) %tuple.454), branch_computations={%region_26.26_spmd, %region_27.30_spmd} | conditional | flops 472043552 | bytes 3831667 | solution.py:107
  895.7 26.2 %while.146 = (s32[]{:T(128)}, f32[4,24,2560]{2,1,0:T(8,128)S(1)}, s32[]{:T(128)}, pred[]{:T(512)}, bf16[5,640,2560]{2,1,0:T(8,128)(2,1)}, /*index=5*/f32[24,640]...) while((s32[]{:T(128)}, f32[4,24,2560]{2,1,0:T(8,128)S(1)}, ...), condition=%wide.region_30.29_spmd, body=%wide.region_28.28_spmd.sunk | while | flops 472043552 | bytes 3831538 | solution.py:86
  902.3 3.9 fusion.172
  907.6 3.9 fusion.172
  924.2 104.4 %all-reduce.9.cloned.1.call-done = f32[1,24,2560]{2,1,0:T(8,128)} async-done(((f32[1,24,2560]{2,1,0:T(8,128)}), f32[1,24,2560]{2,1,0:T(8,128)}) %all-reduce.9.cloned.1.call-update) | async-done | bytes 245776 | tf_op jit(solution)/shard_map/while/body/eval_jaxpr/psum | solution.py:28
  1028.5 4.8 fusion.155
  1033.3 10.2 all_gather.44
  1045.8 130.8 %all-reduce.9.cloned.1.call-done = f32[1,24,2560]{2,1,0:T(8,128)} async-done(((f32[1,24,2560]{2,1,0:T(8,128)}), f32[1,24,2560]{2,1,0:T(8,128)}) %all-reduce.9.cloned.1.call-update) | async-done | bytes 245776 | tf_op jit(solution)/shard_map/while/body/eval_jaxpr/psum | solution.py:28
  1176.6 4.8 fusion.155
  1181.4 10.2 all_gather.44
  1193.9 130.5 %all-reduce.9.cloned.1.call-done = f32[1,24,2560]{2,1,0:T(8,128)} async-done(((f32[1,24,2560]{2,1,0:T(8,128)}), f32[1,24,2560]{2,1,0:T(8,128)}) %all-reduce.9.cloned.1.call-update) | async-done | bytes 245776 | tf_op jit(solution)/shard_map/while/body/eval_jaxpr/psum | solution.py:28
  1324.4 4.8 fusion.155
  1329.2 10.2 all_gather.44
  1339.4 26.2 %conditional.16 = (f32[4,24,2560]{2,1,0:T(8,128)S(1)}) conditional(s32[]{:T(128)} %convert_element_type.157, f32[4,24,2560]{2,1,0:T(8,128)S(1)} %get-tuple-element.2510, (s32[]{:T(128)}, s32[]{:T(128)}, bf16[5,640,2560]{2,1,0:T(8,128)(2,1)}, f32[24,640]{1,0:T(8,128)S(1)}, f32[4,24,2560]{2,1,0:T(8,128)S(1)}) %tuple.454), branch_computations={%region_26.26_spmd, %region_27.30_spmd} | conditional | flops 472043552 | bytes 3831667 | solution.py:107
  1339.4 26.2 %while.146 = (s32[]{:T(128)}, f32[4,24,2560]{2,1,0:T(8,128)S(1)}, s32[]{:T(128)}, pred[]{:T(512)}, bf16[5,640,2560]{2,1,0:T(8,128)(2,1)}, /*index=5*/f32[24,640]...) while((s32[]{:T(128)}, f32[4,24,2560]{2,1,0:T(8,128)S(1)}, ...), condition=%wide.region_30.29_spmd, body=%wide.region_28.28_spmd.sunk | while | flops 472043552 | bytes 3831538 | solution.py:86
  1340.8 3.9 fusion.172
  1356.5 3.9 fusion.172
  1367.8 7.5 all-to-all-start.2
  1375.3 10.2 all-to-all-done.2
  1385.9 9.0 while.151
  1394.9 243.1 %while.152 = (s32[]{:T(128)}, f32[2,24,1024]{2,1,0:T(8,128)S(1)}, f32[2,24,256]{2,1,0:T(8,128)S(1)}, s32[]{:T(128)}, f32[2,24,1024]{2,1,0:T(8,128)S(1)}, /*index...) while((s32[]{:T(128)}, f32[2,24,1024]{2,1,0:T(8,128)S(1)}, ...), condition=%wide.region_46.47_spmd, body=%wide.region_36.46_spmd.sunk | while | flops 151197776 | bytes 4171105 | solution.py:114
  1397.9 97.3 %all-reduce.11.cloned.1.call-done = f32[2,24,1024]{2,1,0:T(8,128)} async-done(((f32[2,24,1024]{2,1,0:T(8,128)}), f32[2,24,1024]{2,1,0:T(8,128)}) %all-reduce.11.cloned.1.call-update) | async-done | bytes 196624 | tf_op jit(solution)/shard_map/while/body/eval_jaxpr/psum | solution.py:28
  1496.7 9.3 all_gather.45
  1506.0 7.3 conditional.17
  1506.0 7.3 while.147
  1517.1 102.2 %all-reduce.11.cloned.1.call-done = f32[2,24,1024]{2,1,0:T(8,128)} async-done(((f32[2,24,1024]{2,1,0:T(8,128)}), f32[2,24,1024]{2,1,0:T(8,128)}) %all-reduce.11.cloned.1.call-update) | async-done | bytes 196624 | tf_op jit(solution)/shard_map/while/body/eval_jaxpr/psum | solution.py:28
  1620.6 9.3 all_gather.45
  1630.0 7.3 conditional.17
  1630.0 7.3 while.147
  (204 shorter events, 108.0 us)
Async XLA Ops:
  9.5 258.9 %all-to-all-start = ((s32[32,1,1]{2,1,0:T(1,128)}), s32[32,1,1]{2,1,0:T(1,128)S(1)}, u32[]{:S(2)}, u32[]{:S(2)}) async-start(s32[32,1,1]{2,1,0:T(1,128)} %copy.27), calls=%async_computation | async-start | bytes 32768 | tf_op jit(solution)/shard_map/all_to_all | solution.py:189
  19.2 7.6 copy-start.8
  19.2 7.7 copy-start
  19.2 7.7 copy-start.7
  26.9 114.2 %all-reduce.5.cloned.1.call-start = ((), (), s32[]{:S(2)}) async-start(), calls=%async_computation.3 | async-start | bytes 393216 | tf_op jit(solution)/shard_map/while/body/eval_jaxpr/psum | solution.py:28
  38.4 0.7 copy-start.1
  143.4 112.8 %all-reduce.5.cloned.1.call-start = ((), (), s32[]{:S(2)}) async-start(), calls=%async_computation.3 | async-start | bytes 393216 | tf_op jit(solution)/shard_map/while/body/eval_jaxpr/psum | solution.py:28
  154.4 0.7 copy-start.1
  266.9 18.1 %copy-start.5 = (f32[1,2,24,640]{3,2,1,0:T(8,128)S(1)}, f32[1,2,24,640]{3,2,1,0:T(8,128)}, u32[]{:S(2)}) copy-start(f32[1,2,24,640]{3,2,1,0:T(8,128)} %param.68) | copy-start | bytes 368644
  266.9 18.1 %copy-start.9 = (s32[3]{0:T(128)S(1)}, s32[3]{0:T(128)}, u32[]{:S(2)}) copy-start(s32[3]{0:T(128)} %constant.1218.clone.1) | copy-start | bytes 40
  268.4 16.1 all-to-all-start.1
  284.9 114.9 %all-reduce.7.cloned.1.call-start = ((), (), s32[]{:S(2)}) async-start(), calls=%async_computation.4 | async-start | bytes 491520 | tf_op jit(solution)/shard_map/while/body/eval_jaxpr/psum | solution.py:28
  406.2 121.1 %all-reduce.7.cloned.1.call-start = ((), (), s32[]{:S(2)}) async-start(), calls=%async_computation.4 | async-start | bytes 491520 | tf_op jit(solution)/shard_map/while/body/eval_jaxpr/psum | solution.py:28
  533.6 116.6 %all-reduce.7.cloned.1.call-start = ((), (), s32[]{:S(2)}) async-start(), calls=%async_computation.4 | async-start | bytes 491520 | tf_op jit(solution)/shard_map/while/body/eval_jaxpr/psum | solution.py:28
  656.4 116.3 %all-reduce.7.cloned.1.call-start = ((), (), s32[]{:S(2)}) async-start(), calls=%async_computation.4 | async-start | bytes 491520 | tf_op jit(solution)/shard_map/while/body/eval_jaxpr/psum | solution.py:28
  774.4 1.0 copy-start.3
  775.5 105.2 %all-reduce.9.cloned.1.call-start = ((), (), s32[]{:S(2)}) async-start(), calls=%async_computation.5 | async-start | bytes 491520 | tf_op jit(solution)/shard_map/while/body/eval_jaxpr/psum | solution.py:28
  922.6 105.9 %all-reduce.9.cloned.1.call-start = ((), (), s32[]{:S(2)}) async-start(), calls=%async_computation.5 | async-start | bytes 491520 | tf_op jit(solution)/shard_map/while/body/eval_jaxpr/psum | solution.py:28
  1044.2 132.4 %all-reduce.9.cloned.1.call-start = ((), (), s32[]{:S(2)}) async-start(), calls=%async_computation.5 | async-start | bytes 491520 | tf_op jit(solution)/shard_map/while/body/eval_jaxpr/psum | solution.py:28
  1192.3 132.1 %all-reduce.9.cloned.1.call-start = ((), (), s32[]{:S(2)}) async-start(), calls=%async_computation.5 | async-start | bytes 491520 | tf_op jit(solution)/shard_map/while/body/eval_jaxpr/psum | solution.py:28
  1366.3 19.6 %copy-start.4 = (f32[2,24,640]{2,1,0:T(8,128)}, f32[2,24,640]{2,1,0:T(8,128)S(1)}, u32[]{:S(2)}) copy-start(f32[2,24,640]{2,1,0:T(8,128)S(1)} %get-tuple-element.1773) | copy-start | bytes 368644
  1367.8 17.7 %all-to-all-start.2 = ((f32[32,1,24,128]{3,2,1,0:T(8,128)}), f32[32,1,24,128]{3,2,1,0:T(8,128)S(1)}, u32[]{:S(2)}, u32[]{:S(2)}) async-start(f32[32,1,24,128]{3,2,1,0:T(8,128)} %copy.32), calls=%async_computation.2 | async-start | bytes 786432 | tf_op jit(solution)/shard_map/all_to_all | solution.py:215
  1394.9 100.3 %all-reduce.11.cloned.1.call-start = ((), (), s32[]{:S(2)}) async-start(), calls=%async_computation.6 | async-start | bytes 393216 | tf_op jit(solution)/shard_map/while/body/eval_jaxpr/psum | solution.py:28
  1396.4 0.7 copy-start.2
  1514.0 105.2 %all-reduce.11.cloned.1.call-start = ((), (), s32[]{:S(2)}) async-start(), calls=%async_computation.6 | async-start | bytes 393216 | tf_op jit(solution)/shard_map/while/body/eval_jaxpr/psum | solution.py:28
  1515.6 0.7 copy-start.2
  1638.0 0.6 copy-start.6
Sparse Core Ops, SparseCore 0:
  39.2 101.9 all-reduce.4
  155.2 100.9 all-reduce.4
  299.4 100.4 all-reduce.6
  420.6 106.6 all-reduce.6
  548.0 102.0 all-reduce.6
  670.8 101.8 all-reduce.6
  779.6 101.0 all-reduce.8
  926.7 101.7 all-reduce.8
  1048.3 128.2 all-reduce.8
  1196.1 128.2 all-reduce.8
  1399.4 95.7 all-reduce.10
  1518.2 100.9 all-reduce.10
where the time goes:
time: 1650 us
  waiting for transfers between devices  1300 us (79%)
  blocking collectives  119 us (7%)
  matrix products  116 us (7%)
  other arithmetic  53.3 us (3%)
  starting transfers between devices  23.6 us (1%)
  local copies, waits for them, and re-layouts  17.8 us (1%)
    psum x12, waiting for transfers between devices, across_front(): return lax.psum(stacked, 'front')  1280 us
    all_gather x12, blocking collectives, across_blk(): pieces = lax.all_gather(partial_rows, 'blk', axis=0, tiled=True)  119 us
    dot_general x24, matrix products, times_tile(): return jnp.dot(vector, tile.astype(jnp.float32), precision=exact_mode)  69.7 us
    dot_general x12, matrix products, times_tile_transposed(): lax.dot_general(vector, tile.astype(jnp.float32), (((1,), (1,)), ((), ())...  45.2 us
    another operation x35, other arithmetic  35.6 us
  transfers between devices with their start and end apart: 15, of which 14 were waited for; matrix products, arithmetic and copies ran while one was open for 2% of the time, Pallas kernels for 0%

commit v1 on v0

v1 whole, which is shorter than its diff:
```python
import functools
import types

import jax
import jax.numpy as jnp
from jax import lax
from jax.experimental import pallas as pl
from jax.experimental.pallas import tpu as pltpu
from jax.sharding import PartitionSpec as P

LANES = 128
MESH = pl.DeviceIdType.MESH
ROOT_PANELS = 4

BACK_2, BACK_1, BACK_0, EARLY_1, EARLY_0 = 4, 5, 6, 7, 8
ROOT_SOURCES = (0, 1, 1, 0, 0, 1, 1, 0, 0)
ROOT_TARGETS = (None, None, 0, 0, 1, 1, 0)
ROOT_ROWS = (0, 1, 1, 0, 0, 1, 1, 0)
CHILD_SUMS, CHILD_ROWS = 4, 3


def loop(count, body, start=0):
    lax.fori_loop(start, count, lambda i, c: (body(i), c)[1], 0)


def wait_bytes(ref, sem):
    pltpu.make_async_copy(ref, ref, sem).wait()


def split(value):
    high = value.astype(jnp.bfloat16).astype(jnp.float32)
    return jnp.concatenate([high, value - high], axis=0).astype(jnp.bfloat16)


def lane_block(index, width=LANES):
    if isinstance(index, int):
        return pl.ds(index * width, width)
    return pl.ds(pl.multiple_of(index * width, width), width)


def put(dest, index, value):
    dest[:, lane_block(index)] = split(value)


def fold(product):
    half = product.shape[0] // 2
    return product[:half] + product[half:]


def kernel(
    fronts, blks,
    emap, rside, cside, rt_hbm, ct_hbm, gt_hbm, rout, cout,
    rt, ct, gt, run, xr, xv, xc, xvc, xn, pb, ob, ar, rk, ak, tgs, tgr, zb,
    rows_r, term_r, recv_r, y_r, rows_c, term_c, recv_c, y_c,
    own, place, inv,
    load_sem, blk_s, blk_r, rs_s, rs_r, ag_s, ag_r, x_s, x_r,
):
    f = lax.axis_index("front")
    b = lax.axis_index("blk")
    half = fronts // 2
    p = f // half
    q = f % half
    directions = rside.shape[1]
    g3 = directions // 8
    root_rb = rside.shape[2] // LANES
    child_rb = cside.shape[2] // LANES
    sends = pb.shape[0]

    def load(src, dst, index):
        return pltpu.make_async_copy(src, dst, load_sem.at[index])

    loads_c = [load(ct_hbm.at[i], ct.at[i], i) for i in range(3)]
    loads_g = [load(gt_hbm.at[i], gt.at[i], 3 + i) for i in range(2)]
    loads_r = [load(rt_hbm.at[i], rt.at[i], 5 + i) for i in range(ROOT_PANELS + 1)]
    for c in loads_c + loads_g + loads_r:
        c.start()

    barrier = pltpu.get_barrier_semaphore()
    loop(fronts, lambda i: pl.semaphore_signal(
        barrier, inc=1, device_id=((f + i) % fronts, b), device_id_type=MESH), 1)
    loop(blks, lambda i: pl.semaphore_signal(
        barrier, inc=1, device_id=(f, (b + i) % blks), device_id_type=MESH), 1)

    def remote(src, dst, ss, rs, device):
        pltpu.make_async_remote_copy(
            src_ref=src, dst_ref=dst, send_sem=ss, recv_sem=rs, device_id=device, device_id_type=MESH
        ).start()

    root = types.SimpleNamespace(
        rows=rows_r, term=term_r, recv=recv_r, y=y_r, blk0=0, rs0=0, ag0=0,
        chunks=term_r.shape[1] // 2, base=0, chunk=f, rb=root_rb)
    child = types.SimpleNamespace(
        rows=rows_c, term=term_c, recv=recv_c, y=y_c, blk0=len(ROOT_ROWS), rs0=len(ROOT_SOURCES),
        ag0=len(ROOT_TARGETS), chunks=term_c.shape[1] // 2, base=p * half, chunk=q, rb=child_rb)

    def mine(side):
        return side.chunk < side.chunks

    def send_rows(side, phase, i):
        ref = side.rows.at[phase, b, i]
        for d in range(1, blks):
            remote(ref, ref, blk_s.at[side.blk0 + phase], blk_r.at[side.blk0 + phase], (f, (b + d) % blks))

    def rows_product(x, tile, slot, i):
        w = tile[slot, pl.ds(pl.multiple_of(i * LANES, LANES), LANES), :]
        return fold(lax.dot_general(x, w, (((1,), (1,)), ((), ())), preferred_element_type=jnp.float32))

    def rows_out(side, phase, x_ref, tile, slot, base):
        def body(i):
            product = rows_product(x_ref[...], tile, slot, i)
            side.rows[phase, b, i] = base(i, product)
            send_rows(side, phase, i)
        loop(side.rb, body)

    def rows_in(side, phase, use):
        wait_bytes(side.rows.at[phase, pl.ds(0, blks - 1)], blk_r.at[side.blk0 + phase])
        for i in range(side.rb):
            total = side.rows[phase, 0, i]
            for s in range(1, blks):
                total = total + side.rows[phase, s, i]
            use(i, total)

    def send_chunk(side, phase, ch):
        owner = side.base + ch
        src = side.term.at[phase, pl.ds(2 * ch, 2)]

        @pl.when(owner == f)
        def _():
            side.recv[phase, q] = src[...]

        @pl.when(owner != f)
        def _():
            remote(src, side.recv.at[phase, q], rs_s.at[side.rs0 + phase], rs_r.at[side.rs0 + phase], (owner, b))

    def cols_out(side, phase, x_ref, tile, slot, add=False, send=True):
        width = min(2 * LANES, tile.shape[2])
        steps = tile.shape[2] // width
        per = width // LANES * g3 // 2

        def body(i):
            c = (i + q) % steps
            w = tile[slot, :, lane_block(c, width)]
            product = fold(jnp.dot(x_ref[...], w, preferred_element_type=jnp.float32))
            for j in range(width // LANES):
                at = pl.ds((c * (width // LANES) + j) * g3, g3)
                value = product[:, j * LANES:(j + 1) * LANES].reshape(g3, 8, LANES)
                if add:
                    value = value + side.term[phase, at]
                side.term[phase, at] = value
            if send:
                for j in range(per):
                    send_chunk(side, phase, c * per + j)
        loop(steps, body)

    def take(side, phase, source=None):
        sem = rs_r.at[side.rs0 + phase]

        def some(count):
            wait_bytes(side.recv.at[phase, pl.ds(0, count)], sem)
        if source is None:
            some(half - 1)
        else:
            pl.when(p == source)(lambda: some(half - 1))
            pl.when(p != source)(lambda: some(half))
        total = side.recv[phase, 0]
        for s in range(1, half):
            total = total + side.recv[phase, s]
        return total

    def spread(side, phase, value, target=None):
        at = pl.ds(2 * side.chunk, 2)
        ref = side.y.at[phase, at]
        side.y[phase, at] = value
        sems = (ag_s.at[side.ag0 + phase], ag_r.at[side.ag0 + phase])
        if side is child:
            loop(half, lambda i: remote(ref, ref, *sems, (side.base + (q + i) % half, b)), 1)
        elif target is None:
            loop(fronts, lambda i: remote(ref, ref, *sems, ((f + i) % fronts, b)), 1)
        else:
            def body(i):
                peer = target * half + (q + i) % half
                pl.when(peer != f)(lambda: remote(ref, ref, *sems, (peer, b)))
            loop(half, body)

    def gather(side, phase, dest):
        def some(count):
            wait_bytes(side.y.at[phase, pl.ds(0, 2 * count)], ag_r.at[side.ag0 + phase])
        pl.when(mine(side))(lambda: some(side.chunks - 1))
        pl.when(jnp.logical_not(mine(side)))(lambda: some(side.chunks))

        def body(c):
            put(dest, c, side.y[phase, pl.ds(c * g3, g3)].reshape(directions, LANES))
        loop(2 * side.chunks // g3, body)

    def own_y(side, phase):
        return side.y[phase, pl.ds(2 * side.chunk, 2)]

    def lanes(i):
        return slice(i * LANES, (i + 1) * LANES)

    lead = (b == 0).astype(jnp.float32)

    for i in range(child_rb):
        put(xc, i, cside[0, :, lanes(i)])

    panel_blocks = half * root_rb

    def route(s):
        r = emap[s]
        k = lax.div(r, panel_blocks)
        within = lax.rem(r, panel_blocks)
        low = jnp.minimum(k, ROOT_PANELS - 1 - k)
        own[s] = half * low + lax.div(within, root_rb)
        place[s] = jnp.where(k == low, 0, root_rb) + lax.rem(within, root_rb)
    loop(sends, route)

    def invert(u):
        index = jnp.int32(0)
        tag = jnp.int32(-1)
        for s in range(sends):
            match = own[s] == u
            index = jnp.where(match, s, index)
            tag = jnp.where(match, place[s], tag)
        inv[u] = index
        tgs[u] = jnp.full((8, LANES), tag, jnp.int32)
    loop(fronts, invert)

    pl.semaphore_wait(barrier, fronts - 1 + blks - 1)

    loads_c[0].wait()
    cols_out(child, 0, xc, ct, 0)

    tgr[f] = tgs[f]

    def send_tag(i):
        u = (f + i) % fronts
        remote(tgs.at[u], tgr.at[f], x_s.at[0], x_r.at[0], (u, b))
    loop(fronts, send_tag, 1)

    def child_step(phase, base=None):
        @pl.when(mine(child))
        def _():
            total = take(child, phase)
            if base is not None:
                total = own_y(child, base) - total
            spread(child, phase, total)

    child_step(0)
    loads_c[1].wait()
    loads_c[2].wait()
    gather(child, 0, xvc)
    for i in range(child_rb):
        run[0, i] = lead * cside[1, :, lanes(i)]
    rows_out(child, 0, xvc, ct, 1, lambda i, d: run[0, i] - d)

    loads_g[0].wait()
    loads_g[1].wait()

    def first_update(s):
        pb[s] = rows_product(xvc[...], gt, 0, s)
    loop(sends, first_update)

    rows_in(child, 0, lambda i, v: put(xc, i, v))
    cols_out(child, 1, xc, ct, 2)
    child_step(1)
    gather(child, 1, xvc)

    def second_update(s):
        pb[s] = pb[s] + rows_product(xvc[...], gt, 1, s)
    loop(sends, second_update)

    ar[f] = pb[inv[f]].reshape(g3, 8, LANES)

    def send_block(i):
        u = (f + i) % fronts
        ob[u] = pb[inv[u]].reshape(g3, 8, LANES)
        remote(ob.at[u], ar.at[f], x_s.at[1], x_r.at[1], (u, b))
    loop(fronts, send_block, 1)
    for l in loads_r:
        l.wait()
    wait_bytes(tgr.at[pl.ds(0, fronts - 1)], x_r.at[0])
    wait_bytes(ar.at[pl.ds(0, fronts - 1)], x_r.at[1])

    def land(u, totals):
        block = ar[u]
        tag = tgr[u][None]
        return tuple(t + jnp.where(tag == s, block, 0.0) for s, t in enumerate(totals))
    zero = jnp.zeros((g3, 8, LANES), jnp.float32)
    landed = lax.fori_loop(0, fronts, land, (zero,) * (2 * root_rb))
    for h in range(2):
        for i in range(root_rb):
            run[h, i] = lead * rside[h, :, lanes(i)] - landed[h * root_rb + i].reshape(directions, LANES)

    def on(pair, body):
        pl.when(p == pair)(body)

    def root_step(phase, out, base=None, early=None):
        @pl.when(mine(root))
        def _():
            total = take(root, phase, ROOT_SOURCES[phase])
            if early is not None:
                total = total + take(root, early, ROOT_SOURCES[early])
            if base is not None:
                total = own_y(root, base) - total
            spread(root, out, total, ROOT_TARGETS[out])

    def from_run(h):
        return lambda i, d: run[h, i] - d

    def subtract(slot):
        def body(i):
            run[1, i] = run[1, i] - rows_product(xv[...], rt, slot, i)
        loop(root_rb, body)

    def solve_rows(phase, slot):
        rows_in(root, phase, lambda i, v: put(xr, i, v))
        cols_out(root, phase, xr, rt, slot)

    def finish_rows(phase, h):
        def use(i, v):
            zb[h * root_rb + i] = v.reshape(g3, 8, LANES)
            rout[h, :, lanes(i)] = v
            put(xr, i, v)
        rows_in(root, phase, use)

    @functools.partial(on, 0)
    def _():
        def body(i):
            rows_r[0, b, i] = run[0, i]
            send_rows(root, 0, i)
        loop(root_rb, body)
        solve_rows(0, 0)
    root_step(0, 0)
    gather(root, 0, xv)

    @functools.partial(on, 1)
    def _():
        rows_out(root, 1, xv, rt, 0, from_run(0))
        subtract(2)
        solve_rows(1, 1)

    on(0, lambda: subtract(1))
    root_step(1, 1)
    gather(root, 1, xv)

    @functools.partial(on, 1)
    def _():
        rows_out(root, 2, xv, rt, 3, from_run(1))
        solve_rows(2, 4)

    on(0, lambda: subtract(2))
    root_step(2, 2)

    @functools.partial(on, 0)
    def _():
        gather(root, 2, xv)
        rows_out(root, 3, xv, rt, 3, from_run(1))
        solve_rows(3, 4)
    root_step(3, 3)

    @functools.partial(on, 0)
    def _():
        gather(root, 3, xv)
        rows_out(root, 4, xv, rt, 4, lambda i, d: d)
        finish_rows(4, 1)
        cols_out(root, BACK_2, xr, rt, 3)
    root_step(BACK_2, 4, base=2)

    @functools.partial(on, 0)
    def _():
        cols_out(root, EARLY_1, xr, rt, 2)
        cols_out(root, EARLY_0, xr, rt, 1)

    @functools.partial(on, 1)
    def _():
        gather(root, 4, xv)
        rows_out(root, 5, xv, rt, 4, lambda i, d: d)
        finish_rows(5, 1)
        cols_out(root, BACK_1, xr, rt, 3)
    root_step(BACK_1, 5, base=1, early=EARLY_1)

    @functools.partial(on, 1)
    def _():
        cols_out(root, BACK_0, xr, rt, 2, send=False)
        gather(root, 5, xv)
        rows_out(root, 6, xv, rt, 1, lambda i, d: d)
        finish_rows(6, 0)
        cols_out(root, BACK_0, xr, rt, 0, add=True)
    root_step(BACK_0, 6, base=0, early=EARLY_0)

    @functools.partial(on, 0)
    def _():
        gather(root, 6, xv)
        rows_out(root, 7, xv, rt, 0, lambda i, d: d)
        finish_rows(7, 0)

    def answer(u):
        tag = tgr[u][None]
        block = jnp.where(tag == 0, zb[0], 0.0)
        for s in range(1, 2 * root_rb):
            block = jnp.where(tag == s, zb[s], block)
        return block

    def send_answer(i):
        u = (f + i) % fronts
        rk[u] = answer(u)
        remote(rk.at[u], ak.at[f], x_s.at[2], x_r.at[2], (u, b))
    loop(fronts, send_answer, 1)
    ak[f] = answer(f)
    wait_bytes(ak.at[pl.ds(0, fronts - 1)], x_r.at[2])

    def need(s):
        put(xn, s, ak[own[s]].reshape(directions, LANES))
    loop(sends, need)

    cols_out(child, 2, xn, gt, 1)
    child_step(2, base=1)
    cols_out(child, 3, xn, gt, 0, send=False)
    gather(child, 2, xvc)
    rows_out(child, 1, xvc, ct, 2, lambda i, d: d)

    def last(h):
        def use(i, v):
            cout[h, :, lanes(i)] = v
            put(xc, i, v)
        return use
    rows_in(child, 1, last(1))
    cols_out(child, 3, xc, ct, 1, add=True)
    child_step(3, base=0)
    gather(child, 3, xvc)
    rows_out(child, 2, xvc, ct, 0, lambda i, d: d)
    rows_in(child, 2, last(0))

    def sent_chunks(side, phase, count):
        wait_bytes(side.term.at[phase, pl.ds(0, 2 * count)], rs_s.at[side.rs0 + phase])

    def both(condition, yes, no):
        pl.when(condition)(yes)
        pl.when(jnp.logical_not(condition))(no)

    for side, phases in ((root, len(ROOT_SOURCES)), (child, CHILD_SUMS)):
        for phase in range(phases):
            def sums(side=side, phase=phase):
                both(mine(side), lambda: sent_chunks(side, phase, side.chunks - 1),
                     lambda: sent_chunks(side, phase, side.chunks))
            if side is root:
                on(ROOT_SOURCES[phase], sums)
            else:
                sums()
    for phase, pair in enumerate(ROOT_ROWS):
        on(pair, lambda phase=phase: wait_bytes(rows_r.at[phase, pl.ds(0, blks - 1)], blk_s.at[phase]))
    for phase in range(CHILD_ROWS):
        wait_bytes(rows_c.at[phase, pl.ds(0, blks - 1)], blk_s.at[child.blk0 + phase])

    @pl.when(mine(root))
    def _():
        for phase, target in enumerate(ROOT_TARGETS):
            if target is None:
                wait_bytes(ob.at[pl.ds(0, fronts - 1), pl.ds(0, 2)], ag_s.at[phase])
            else:
                both(p == target,
                     lambda phase=phase: wait_bytes(tgr.at[pl.ds(0, 2 * (half - 1))], ag_s.at[phase]),
                     lambda phase=phase: wait_bytes(tgr.at[pl.ds(0, 2 * half)], ag_s.at[phase]))

    @pl.when(mine(child))
    def _():
        for phase in range(CHILD_SUMS):
            wait_bytes(tgr.at[pl.ds(0, 2 * (half - 1))], ag_s.at[child.ag0 + phase])
    wait_bytes(tgs.at[pl.ds(0, fronts - 1)], x_s.at[0])
    wait_bytes(ob.at[pl.ds(0, fronts - 1)], x_s.at[1])
    wait_bytes(rk.at[pl.ds(0, fronts - 1)], x_s.at[2])


def on_device(fronts, blks, root_tiles, child_tiles, child_update, extend_map, root_side, child_side):
    root, child = root_tiles[0], child_tiles[0]
    rside, cside = root_side[0], child_side[0]
    update = jnp.transpose(child_update, (1, 0, 2))
    directions = rside.shape[1]
    half = fronts // 2
    g3 = directions // 8
    root_rb, child_rb = rside.shape[2] // LANES, cside.shape[2] // LANES
    root_cols, child_cols = root.shape[2], child.shape[2]
    root_tiles8, child_tiles8 = root_cols // LANES * g3, child_cols // LANES * g3
    sends = extend_map.shape[0]
    f32, bf16 = jnp.float32, jnp.bfloat16
    vmem, sem = pltpu.VMEM, pltpu.SemaphoreType.DMA
    sums, rows, casts = len(ROOT_SOURCES), len(ROOT_ROWS), len(ROOT_TARGETS)
    whole = pl.BlockSpec(memory_space=pltpu.VMEM)
    hbm = pl.BlockSpec(memory_space=pl.ANY)
    outs = pl.pallas_call(
        functools.partial(kernel, fronts, blks),
        out_shape=(jax.ShapeDtypeStruct(rside.shape, f32), jax.ShapeDtypeStruct(cside.shape, f32)),
        in_specs=[pl.BlockSpec(memory_space=pltpu.SMEM), whole, whole, hbm, hbm, hbm],
        out_specs=(whole, whole),
        scratch_shapes=[
            vmem(root.shape, bf16), vmem(child.shape, bf16), vmem(update.shape, bf16),
            vmem((2, root_rb, directions, LANES), f32),
            vmem((2 * directions, rside.shape[2]), bf16), vmem((2 * directions, root_cols), bf16),
            vmem((2 * directions, cside.shape[2]), bf16), vmem((2 * directions, child_cols), bf16),
            vmem((2 * directions, sends * LANES), bf16),
            vmem((sends, directions, LANES), f32),
            vmem((fronts, g3, 8, LANES), f32), vmem((fronts, g3, 8, LANES), f32),
            vmem((fronts, g3, 8, LANES), f32), vmem((fronts, g3, 8, LANES), f32),
            vmem((fronts, 8, LANES), jnp.int32), vmem((fronts, 8, LANES), jnp.int32),
            vmem((2 * root_rb, g3, 8, LANES), f32),
            vmem((rows, blks, root_rb, directions, LANES), f32), vmem((sums, root_tiles8, 8, LANES), f32),
            vmem((sums, half, 2, 8, LANES), f32), vmem((casts, root_tiles8, 8, LANES), f32),
            vmem((CHILD_ROWS, blks, child_rb, directions, LANES), f32),
            vmem((CHILD_SUMS, child_tiles8, 8, LANES), f32),
            vmem((CHILD_SUMS, half, 2, 8, LANES), f32), vmem((CHILD_SUMS, child_tiles8, 8, LANES), f32),
            pltpu.SMEM((sends,), jnp.int32), pltpu.SMEM((sends,), jnp.int32),
            pltpu.SMEM((fronts,), jnp.int32),
            sem((3 + 2 + root.shape[0],)),
            sem((rows + CHILD_ROWS,)), sem((rows + CHILD_ROWS,)),
            sem((sums + CHILD_SUMS,)), sem((sums + CHILD_SUMS,)),
            sem((casts + CHILD_SUMS,)), sem((casts + CHILD_SUMS,)),
            sem((3,)), sem((3,)),
        ],
        compiler_params=pltpu.CompilerParams(
            collective_id=0, has_side_effects=True, vmem_limit_bytes=58 * 1024 * 1024
        ),
    )(extend_map, rside, cside, root, child, update)
    return (outs[0][None], outs[1][None])


def solution(mesh):
    in_specs = (
        P("front", None, None, "blk"),
        P("front", None, None, "blk"),
        P("front", None, "blk"),
        P("front"),
        P("front", None, None, None),
        P("front", None, None, None),
    )
    out_specs = (P("front", None, None, None), P("front", None, None, None))
    body = functools.partial(on_device, mesh.shape["front"], mesh.shape["blk"])
    return jax.shard_map(body, mesh=mesh, in_specs=in_specs, out_specs=out_specs, check_vma=False)
```

time: 1650 us -> 220 us (0.13)
  waiting for transfers between devices: 1300 us -> 0 us
  Pallas kernels: 0 us -> 208 us
  blocking collectives: 119 us -> 0 us
  matrix products: 116 us -> 0 us
  other arithmetic: 53.3 us -> 0 us
  starting transfers between devices: 23.6 us -> 0 us
    psum x12 -> x0, waiting for transfers between devices: 1280 us -> none  [across_front(): return lax.psum(stacked, 'front')]
    pallas_call x0 -> x1, Pallas kernels: none -> 208 us  [on_device(): pl.pallas_call(functools.partial(kernel, fronts, blks), out_shape=(jax.Sh...]
    all_gather x12 -> x0, blocking collectives: 119 us -> none  [across_blk(): pieces = lax.all_gather(partial_rows, 'blk', axis=0, tiled=True)]
    dot_general x40 -> x0, matrix products: 116 us -> none  [the longest x24 69.7 us: times_tile(): return jnp.dot(vector, tile.astype(jnp.float32), precision=exact_mode)]
    another operation x35 -> x0, other arithmetic: 35.6 us -> none
    all_to_all x3 -> x0, starting transfers between devices: 23.1 us -> none  [the longest x1 9.6 us: on_device(): lax.all_to_all(slot_tags.reshape(fronts, capacity), 'front', split_axis=0...]
    all_to_all x3 -> x0, waiting for transfers between devices: 19.7 us -> none  [the longest x1 10.2 us: on_device(): lax.all_to_all(returning, 'front', split_axis=0, concat_axis=0, tiled=True)]
  transfers between devices with their start and end apart: 15 -> 0, of which waited for: 14 -> 0; matrix products, arithmetic and copies ran while one was open for 2% -> 0% of each run, Pallas kernels for 0% -> 0%
where the time goes in v1:
time: 220 us; the launch traced here: 219 us
  Pallas kernels  208 us (95%)
  local copies, waits for them, and re-layouts  10.4 us (5%)
    pallas_call x1, Pallas kernels, on_device(): pl.pallas_call(functools.partial(kernel, fronts, blks), out_shape=(jax.Sh...  208 us
    unnamed x3, local copies, waits for them, and re-layouts  10.4 us

profile of v1, /device:TPU:1, one launch (start us, length us, event | category | flops | bytes accessed | tf_op | source)
XLA Modules:
  0.0 219.4 jit_solution(1766568208179281304)
XLA Ops:
  0.6 7.4 %copy.10 = bf16[1536,2,1024]{2,0,1:T(8,128)(2,1)} copy(bf16[1536,2,1024]{2,1,0:T(2,128)(2,1)} %param.8) | data formatting | bytes 12582912 | tf_op args[2]
  8.1 208.3 %shard_map.77 = (f32[2,24,640]{2,1,0:T(8,128)}, f32[2,24,256]{2,1,0:T(8,128)}) custom-call(s32[12]{0:T(128)} %emap.1, f32[2,24,640]{2,1,0:T(8,128)} %bitcast.12, f32[2,24,256]{2,1,0:T(8,128)} %bitcast.14, bf16[5,640,2560]{2,1,0:T(8,128)(2,1)} %bitcast.10, bf16[3,256,1024]{2,1,0:T(8,128)(2,1)} %bitcast.11, bf16[2,1536,1024]{2,1,0:T(8,128)(2,1)} %bitcast.9), custom_call_target="tpu_custom_call" | custom-call | tf_op jit(solution)/shard_map/pallas_call | solution.py:490
  216.4 1.6 copy.13
  218.0 1.4 copy.14

commit v2 on v0

v2 whole, which is shorter than its diff:
```python
import functools
import types

import jax
import jax.numpy as jnp
from jax import lax
from jax.experimental import pallas as pl
from jax.experimental.pallas import tpu as pltpu
from jax.sharding import PartitionSpec as P

LANES = 128
SUB = 8
MESH = pl.DeviceIdType.MESH
ROOT_PANELS = 4

BACK_2, BACK_1, BACK_0, EARLY_1, EARLY_0 = 4, 5, 6, 7, 8
SUM_FROM = (0, 1, 1, 0, 0, 1, 1, 0, 0)
SUM_AT = (0, 1, 1, 0, 1, 1, 0, 1, 0)
CAST_FROM = (0, 1, 1, 0, 1, 1, 0)
CAST_TO = ((1, 0), (1, 0), (0,), (0,), (1,), (1,), (0,))
ROOT_ROWS = (0, 1, 1, 0, 0, 1, 1, 0)
CHILD_SUMS, CHILD_ROWS = 4, 3


def loop(count, body, start=0):
    lax.fori_loop(start, count, lambda i, c: (body(i), c)[1], 0)


def wait_bytes(ref, sem):
    pltpu.make_async_copy(ref, ref, sem).wait()


def split(value):
    high = value.astype(jnp.bfloat16).astype(jnp.float32)
    return jnp.concatenate([high, value - high], axis=0).astype(jnp.bfloat16)


def fold(product):
    return product[:SUB] + product[SUB:]


def times(x, tile):
    return jnp.dot(x, tile, preferred_element_type=jnp.float32)


def times_transposed(x, tile):
    return lax.dot_general(x, tile, (((1,), (1,)), ((), ())), preferred_element_type=jnp.float32)


def lanes(i):
    return slice(i * LANES, (i + 1) * LANES)


def aligned(index, size):
    return pl.ds(index * size if isinstance(index, int) else pl.multiple_of(index * size, size), size)


def both(condition, yes, no):
    pl.when(condition)(yes)
    pl.when(jnp.logical_not(condition))(no)


def kernel(
    fronts, blks,
    emap, rside, cside, rt_hbm, ct_hbm, gt_hbm, rout, cout,
    rt, ct, gv, gt, shuffle, run, xr, xv, xc, xvc, xn, pb, ob, ar, rk, ak, nk, tgs, tgr, zb,
    rows_r, term_r, recv_r, y_r, rows_c, term_c, recv_c, y_c,
    counts, own, place, inv,
    load_sem, blk_s, blk_r, rs_s, rs_r, ag_s, ag_r, x_s, x_r, t_s, t_r,
):
    f = lax.axis_index("front")
    b = lax.axis_index("blk")
    half = fronts // 2
    p = f // half
    q = f % half
    count_groups = rside.shape[1] // SUB
    root_rb = rside.shape[2] // LANES
    child_rb = cside.shape[2] // LANES
    sends = pb.shape[1]

    def groups(body):
        loop(count_groups, body)

    def load(src, dst, index):
        copy = pltpu.make_async_copy(src, dst, load_sem.at[index])
        copy.start()
        return copy

    loads_c = [load(ct_hbm.at[0], ct.at[0], 0)]
    load_g = load(gt_hbm, gv, 3)
    loads_c += [load(ct_hbm.at[i], ct.at[i], i) for i in (1, 2)]
    loads_r = [load(rt_hbm.at[i], rt.at[i], 4 + i) for i in range(ROOT_PANELS + 1)]

    barrier = pltpu.get_barrier_semaphore()
    loop(fronts, lambda i: pl.semaphore_signal(
        barrier, inc=1, device_id=((f + i) % fronts, b), device_id_type=MESH), 1)
    loop(blks, lambda i: pl.semaphore_signal(
        barrier, inc=1, device_id=(f, (b + i) % blks), device_id_type=MESH), 1)

    def remote(src, dst, ss, rs, device):
        pltpu.make_async_remote_copy(
            src_ref=src, dst_ref=dst, send_sem=ss, recv_sem=rs, device_id=device, device_id_type=MESH
        ).start()

    root = types.SimpleNamespace(
        rows=rows_r, term=term_r, recv=recv_r, y=y_r, blk0=0, rs0=0, ag0=0,
        per=recv_r.shape[3], chunks=term_r.shape[2] // recv_r.shape[3], rb=root_rb, x=xr, v=xv)
    child = types.SimpleNamespace(
        rows=rows_c, term=term_c, recv=recv_c, y=y_c, blk0=len(ROOT_ROWS), rs0=len(SUM_FROM),
        ag0=len(CAST_FROM), per=recv_c.shape[3], chunks=term_c.shape[2] // recv_c.shape[3], rb=child_rb,
        x=xc, v=xvc)

    def member_of(ch, g):
        return (ch + 5 * g) % half

    def chunk_of(member, g):
        return (member + half - 5 * g % half) % half

    def at_pair(side, phase, table):
        return p if side is child else table[phase]

    def mine(side, pair, g):
        holds = chunk_of(q, g) < side.chunks
        return holds if side is child else (p == pair) & holds

    def x_group(x, g):
        return x.at[aligned(g, 2 * SUB)]

    def put(x, g, i, value):
        x[aligned(g, 2 * SUB), lanes(i)] = split(value)

    def send_rows(side, phase, g):
        ref = side.rows.at[phase, g, b]
        sems = (blk_s.at[side.blk0 + phase, g], blk_r.at[side.blk0 + phase, g])
        for d in range(1, blks):
            remote(ref, ref, *sems, (f, (b + d) % blks))

    def rows_out(side, phase, g, tile, slot, base=None):
        product = fold(times_transposed(x_group(side.v, g)[...], tile[slot]))
        for i in range(side.rb):
            value = product[:, lanes(i)]
            side.rows[phase, g, b, i] = value if base is None else base(i) - value
        send_rows(side, phase, g)

    def rows_in(side, phase, g, use=None):
        wait_bytes(side.rows.at[phase, g, pl.ds(0, blks - 1)], blk_r.at[side.blk0 + phase, g])
        for i in range(side.rb):
            total = side.rows[phase, g, 0, i]
            for s in range(1, blks):
                total = total + side.rows[phase, g, s, i]
            if use is not None:
                use(i, total)
            put(side.x, g, i, total)

    def send_chunks(side, phase, g):
        pair = at_pair(side, phase, SUM_AT)
        sems = (rs_s.at[side.rs0 + phase, g], rs_r.at[side.rs0 + phase, g])

        def send(ch):
            owner = pair * half + member_of(ch, g)
            src = side.term.at[phase, g, pl.ds(side.per * ch, side.per)]

            @pl.when(owner == f)
            def _():
                side.recv[phase, g, q] = src[...]

            @pl.when(owner != f)
            def _():
                remote(src, side.recv.at[phase, g, q], *sems, (owner, b))
        loop(side.chunks, send)

    def keep_cols(side, phase, g, product, add, first=0):
        for i in range(product.shape[1] // LANES):
            value = product[:, lanes(i)]
            if add:
                value = value + side.term[phase, g, first + i]
            side.term[phase, g, first + i] = value

    def cols_out(side, phase, g, x, tile, slot, add=False):
        keep_cols(side, phase, g, fold(times(x_group(x, g)[...], tile[slot])), add)
        send_chunks(side, phase, g)

    def cols_whole(side, phase, x, tile, slot):
        width = 4 * LANES if tile.shape[2] % (4 * LANES) == 0 else LANES
        for c in range(tile.shape[2] // width):
            product = times(x[...], tile[slot, :, c * width:(c + 1) * width])
            for g in range(count_groups):
                keep_cols(side, phase, g, fold(product[2 * SUB * g:2 * SUB * (g + 1)]), False, c * width // LANES)

    def take(side, phase, g):
        sem = rs_r.at[side.rs0 + phase, g]

        def some(count):
            wait_bytes(side.recv.at[phase, g, pl.ds(0, count)], sem)
        some(half - 1 if side is child or SUM_AT[phase] == SUM_FROM[phase] else half)
        total = side.recv[phase, g, 0]
        for s in range(1, half):
            total = total + side.recv[phase, g, s]
        return total

    def spread(side, phase, g, value):
        at = pl.ds(side.per * chunk_of(q, g), side.per)
        ref = side.y.at[phase, g, at]
        side.y[phase, g, at] = value
        sems = (ag_s.at[side.ag0 + phase, g], ag_r.at[side.ag0 + phase, g])
        source = at_pair(side, phase, CAST_FROM)
        target = p if side is child else CAST_TO[phase][0]

        def send(i):
            remote(ref, ref, *sems, (target * half + (q + i) % half, b))
        loop(half, send, 1 if side is child or target == source else 0)

    def spread_more(phase, g):
        @pl.when(mine(root, CAST_FROM[phase], g))
        def _():
            ref = root.y.at[phase, g, pl.ds(root.per * chunk_of(q, g), root.per)]
            target = CAST_TO[phase][1]

            def send(i):
                remote(ref, ref, ag_s.at[phase, g], ag_r.at[phase, g], (target * half + (q + i) % half, b))
            loop(half, send, 1 if target == CAST_FROM[phase] else 0)

    def gather(side, phase, g):
        def some(count):
            wait_bytes(side.y.at[phase, g, pl.ds(0, side.per * count)], ag_r.at[side.ag0 + phase, g])
        both(mine(side, at_pair(side, phase, CAST_FROM), g), lambda: some(side.chunks - 1),
             lambda: some(side.chunks))
        for i in range(side.term.shape[2]):
            put(side.v, g, i, side.y[phase, g, i])

    def step(side, phase, out, g, base=None, early=None):
        @pl.when(mine(side, at_pair(side, phase, SUM_AT), g))
        def _():
            total = take(side, phase, g)
            if early is not None:
                total = total + take(side, early, g)
            if base is not None:
                total = side.y[base, g, pl.ds(side.per * chunk_of(q, g), side.per)] - total
            spread(side, out, g, total)

    lead = (b == 0).astype(jnp.float32)

    def side_rows(ref, h, g, i):
        return ref[h, aligned(g, SUB), lanes(i)]

    def put_child(g):
        for i in range(child_rb):
            put(xc, g, i, side_rows(cside, 0, g, i))
    groups(put_child)

    panel_blocks = half * root_rb

    def route(s):
        r = emap[s]
        k = lax.div(r, panel_blocks)
        within = lax.rem(r, panel_blocks)
        low = jnp.minimum(k, ROOT_PANELS - 1 - k)
        own[s] = half * low + lax.div(within, root_rb)
        place[s] = jnp.where(k == low, 0, root_rb) + lax.rem(within, root_rb)

    def invert(u):
        index = jnp.int32(0)
        tag = jnp.int32(-1)
        for s in range(sends):
            match = own[s] == u
            index = jnp.where(match, s, index)
            tag = jnp.where(match, place[s], tag)
        inv[u] = index
        tgs[u] = jnp.full((SUB, LANES), tag, jnp.int32)

    part_rows = 16
    slots = shuffle.shape[0]
    parts = gv.shape[0] // (part_rows * slots)

    def part(n):
        for s in range(slots):
            at = pl.ds(pl.multiple_of((n * slots + s) * part_rows, part_rows), part_rows)
            rows = gv[at].reshape(2 * part_rows, gv.shape[2]).astype(jnp.float32)
            for j in range(gv.shape[2] // LANES):
                shuffle[s, j] = rows[:, lanes(j)]
            for j in range(gv.shape[2] // LANES):
                for k in range(2):
                    gt[k, at, lanes(j)] = shuffle[s, j, pl.ds(k, part_rows, stride=2), :].astype(gt.dtype)

    loads_c[0].wait()
    cols_whole(child, 0, xc, ct, 0)
    loop(sends, route)
    loop(fronts, invert)
    pl.semaphore_wait(barrier, fronts - 1 + blks - 1)
    groups(lambda g: send_chunks(child, 0, g))
    tgr[f] = tgs[f]

    def send_tag(i):
        u = (f + i) % fronts
        remote(tgs.at[u], tgr.at[f], t_s.at[0], t_r.at[0], (u, b))
    loop(fronts, send_tag, 1)
    load_g.wait()
    loop(parts // 2, part)
    groups(lambda g: step(child, 0, 0, g))
    loop(parts, part, parts // 2)
    loads_c[1].wait()
    loads_c[2].wait()

    def child_1(g):
        gather(child, 0, g)
        rows_out(child, 0, g, ct, 1, lambda i: lead * side_rows(cside, 1, g, i))
    groups(child_1)

    def update_0():
        for s in range(0, sends, 2):
            product = times_transposed(xvc[...], gt[0, s * LANES:(s + 2) * LANES])
            for g in range(count_groups):
                rows = fold(product[2 * SUB * g:2 * SUB * (g + 1)])
                for j in range(2):
                    pb[g, s + j] = rows[:, lanes(j)]
    update_0()

    def child_2(g):
        rows_in(child, 0, g)
        cols_out(child, 1, g, xc, ct, 2)
    groups(child_2)
    groups(lambda g: step(child, 1, 1, g))

    def update_1(g):
        gather(child, 1, g)
        for s in range(0, sends, 2):
            rows = fold(times_transposed(x_group(xvc, g)[...], gt[1, s * LANES:(s + 2) * LANES]))
            for j in range(2):
                pb[g, s + j] = pb[g, s + j] + rows[:, lanes(j)]
        ar[g, f] = pb[g, inv[f]]

        def send_block(i):
            u = (f + i) % fronts
            ob[g, u] = pb[g, inv[u]]
            remote(ob.at[g, u], ar.at[g, f], x_s.at[0, g], x_r.at[0, g], (u, b))
        loop(fronts, send_block, 1)
    groups(update_1)
    for l in loads_r:
        l.wait()
    wait_bytes(tgr.at[pl.ds(0, fronts - 1)], t_r.at[0])

    def land(g):
        wait_bytes(ar.at[g, pl.ds(0, fronts - 1)], x_r.at[0, g])

        def add(u, totals):
            block = ar[g, u]
            tag = tgr[u]
            return tuple(t + jnp.where(tag == s, block, 0.0) for s, t in enumerate(totals))
        zero = jnp.zeros((SUB, LANES), jnp.float32)
        landed = lax.fori_loop(0, fronts, add, (zero,) * (2 * root_rb), unroll=4)
        for h in range(2):
            for i in range(root_rb):
                run[g, h, i] = lead * side_rows(rside, h, g, i) - landed[h * root_rb + i]

    def on(pair, body):
        pl.when(p == pair)(body)

    def subtract(slot):
        width = 2 * LANES
        for c in range(0, root_rb * LANES, width):
            size = min(width, root_rb * LANES - c)
            product = times_transposed(xv[...], rt[slot, c:c + size])
            for g in range(count_groups):
                rows = fold(product[2 * SUB * g:2 * SUB * (g + 1)])
                for j in range(size // LANES):
                    run[g, 1, c // LANES + j] = run[g, 1, c // LANES + j] - rows[:, lanes(j)]

    def solve(phase, slot):
        def one(g):
            rows_in(root, phase, g)
            cols_out(root, phase, g, xr, rt, slot)
        groups(one)

    def advance(cast, phase, h, slot):
        def one(g):
            gather(root, cast, g)
            rows_out(root, phase, g, rt, slot, lambda i: run[g, h, i])
        groups(one)

    def retreat(cast, phase, h, slot):
        def one(g):
            gather(root, cast, g)
            rows_out(root, phase, g, rt, slot)
        groups(one)

    def finish(phase, h, after):
        def one(g):
            def use(i, v):
                zb[g, h * root_rb + i] = v
                rout[h, aligned(g, SUB), lanes(i)] = v
            rows_in(root, phase, g, use)
            after(g)
        groups(one)

    def answers(g):
        def answer(u):
            tag = tgr[u]
            block = jnp.where(tag == 0, zb[g, 0], 0.0)
            for s in range(1, 2 * root_rb):
                block = jnp.where(tag == s, zb[g, s], block)
            return block

        def send_answer(i):
            u = (f + i) % fronts
            rk[g, u] = answer(u)
            remote(rk.at[g, u], ak.at[g, f], x_s.at[1, g], x_r.at[1, g], (u, b))
        loop(fronts, send_answer, 1)
        ak[g, f] = answer(f)

    def first(g):
        land(g)

        @pl.when(p == 0)
        def _():
            for i in range(root_rb):
                rows_r[0, g, b, i] = run[g, 0, i]
            send_rows(root, 0, g)
    groups(first)

    @functools.partial(on, 0)
    def _():
        solve(0, 0)
        groups(lambda g: step(root, 0, 0, g))
        groups(lambda g: spread_more(0, g))
        groups(lambda g: gather(root, 0, g))
        subtract(1)
        groups(lambda g: gather(root, 1, g))
        subtract(2)
        advance(2, 3, 1, 3)
        solve(3, 4)
        groups(lambda g: step(root, 3, 3, g))
        retreat(3, 4, 1, 4)
        finish(4, 1, lambda g: cols_out(root, BACK_2, g, xr, rt, 3))
        cols_whole(root, EARLY_1, xr, rt, 2)
        groups(lambda g: send_chunks(root, EARLY_1, g))
        cols_whole(root, EARLY_0, xr, rt, 1)
        groups(lambda g: send_chunks(root, EARLY_0, g))
        groups(lambda g: step(root, BACK_0, 6, g, base=0, early=EARLY_0))
        retreat(6, 7, 0, 0)
        finish(7, 0, lambda g: answers(g))

    @functools.partial(on, 1)
    def _():
        advance(0, 1, 0, 0)
        subtract(2)
        solve(1, 1)
        groups(lambda g: step(root, 1, 1, g))
        advance(1, 2, 1, 3)
        groups(lambda g: spread_more(1, g))
        solve(2, 4)
        groups(lambda g: step(root, 2, 2, g))
        groups(lambda g: step(root, BACK_2, 4, g, base=2))
        retreat(4, 5, 1, 4)
        finish(5, 1, lambda g: cols_out(root, BACK_1, g, xr, rt, 3))
        cols_whole(root, BACK_0, xr, rt, 2)
        groups(lambda g: step(root, BACK_1, 5, g, base=1, early=EARLY_1))
        retreat(5, 6, 0, 1)
        finish(6, 0, lambda g: cols_out(root, BACK_0, g, xr, rt, 0, add=True))
        groups(lambda g: answers(g))

    def child_3(g):
        wait_bytes(ak.at[g, pl.ds(0, fronts - 1)], x_r.at[1, g])

        def keep(u):
            nk[u] = ak[g, u]
        loop(fronts, keep)
        for s in range(sends):
            put(xn, g, s, nk[own[s]])
        cols_out(child, 2, g, xn, gt, 1)
    groups(child_3)
    cols_whole(child, 3, xn, gt, 0)
    groups(lambda g: step(child, 2, 2, g, base=1))

    def child_4(g):
        gather(child, 2, g)
        rows_out(child, 1, g, ct, 2)
    groups(child_4)

    def last(h, g):
        def use(i, v):
            cout[h, aligned(g, SUB), lanes(i)] = v
        return use

    def child_5(g):
        rows_in(child, 1, g, last(1, g))
        cols_out(child, 3, g, xc, ct, 1, add=True)
    groups(child_5)
    groups(lambda g: step(child, 3, 3, g, base=0))

    def child_6(g):
        gather(child, 3, g)
        rows_out(child, 2, g, ct, 0)
    groups(child_6)
    groups(lambda g: rows_in(child, 2, g, last(0, g)))

    def drain(g):
        def sent_chunks(side, phase, count):
            wait_bytes(side.term.at[phase, g, pl.ds(0, side.per * count)], rs_s.at[side.rs0 + phase, g])

        def sent_terms(side, phase, same):
            if same:
                both(mine(side, at_pair(side, phase, SUM_AT), g),
                     lambda: sent_chunks(side, phase, side.chunks - 1),
                     lambda: sent_chunks(side, phase, side.chunks))
            else:
                sent_chunks(side, phase, side.chunks)
        for phase in range(len(SUM_FROM)):
            on(SUM_FROM[phase], lambda phase=phase: sent_terms(root, phase, SUM_FROM[phase] == SUM_AT[phase]))
        for phase in range(CHILD_SUMS):
            sent_terms(child, phase, True)
        for phase, pair in enumerate(ROOT_ROWS):
            on(pair, lambda phase=phase: wait_bytes(rows_r.at[phase, g, pl.ds(0, blks - 1)], blk_s.at[phase, g]))
        for phase in range(CHILD_ROWS):
            wait_bytes(rows_c.at[phase, g, pl.ds(0, blks - 1)], blk_s.at[child.blk0 + phase, g])
        for phase, source in enumerate(CAST_FROM):
            @pl.when(mine(root, source, g))
            def _(phase=phase, source=source):
                count = half * len(CAST_TO[phase]) - (source in CAST_TO[phase])
                wait_bytes(counts.at[pl.ds(0, count)], ag_s.at[phase, g])

        @pl.when(mine(child, None, g))
        def _():
            for phase in range(CHILD_SUMS):
                wait_bytes(recv_c.at[phase, g, pl.ds(0, half - 1)], ag_s.at[child.ag0 + phase, g])
        wait_bytes(ob.at[g, pl.ds(0, fronts - 1)], x_s.at[0, g])
        wait_bytes(rk.at[g, pl.ds(0, fronts - 1)], x_s.at[1, g])
    groups(drain)
    wait_bytes(tgs.at[pl.ds(0, fronts - 1)], t_s.at[0])


def on_device(fronts, blks, root_tiles, child_tiles, child_update, extend_map, root_side, child_side):
    root, child = root_tiles[0], child_tiles[0]
    rside, cside = root_side[0], child_side[0]
    directions = rside.shape[1]
    groups = directions // SUB
    half = fronts // 2
    root_rb, child_rb = rside.shape[2] // LANES, cside.shape[2] // LANES
    root_cols, child_cols = root.shape[2], child.shape[2]
    root_blocks, child_blocks = root_cols // LANES, child_cols // LANES
    update_rows, panels, _ = child_update.shape
    sends = extend_map.shape[0]
    root_per = -(-root_blocks // half)
    child_per = -(-child_blocks // half)
    f32, bf16 = jnp.float32, jnp.bfloat16
    vmem, sem = pltpu.VMEM, pltpu.SemaphoreType.DMA
    sums, rows, casts = len(SUM_FROM), len(ROOT_ROWS), len(CAST_FROM)
    whole = pl.BlockSpec(memory_space=pltpu.VMEM)
    hbm = pl.BlockSpec(memory_space=pl.ANY)
    tile = (SUB, LANES)
    outs = pl.pallas_call(
        functools.partial(kernel, fronts, blks),
        out_shape=(jax.ShapeDtypeStruct(rside.shape, f32), jax.ShapeDtypeStruct(cside.shape, f32)),
        in_specs=[pl.BlockSpec(memory_space=pltpu.SMEM), whole, whole, hbm, hbm, hbm],
        out_specs=(whole, whole),
        scratch_shapes=[
            vmem(root.shape, bf16), vmem(child.shape, bf16), vmem(child_update.shape, bf16),
            vmem((panels, update_rows, child_cols), bf16), vmem((4, child_blocks, 32, LANES), f32),
            vmem((groups, 2, root_rb) + tile, f32),
            vmem((2 * directions, rside.shape[2]), bf16), vmem((2 * directions, root_cols), bf16),
            vmem((2 * directions, cside.shape[2]), bf16), vmem((2 * directions, child_cols), bf16),
            vmem((2 * directions, sends * LANES), bf16),
            vmem((groups, sends) + tile, f32),
            vmem((groups, fronts) + tile, f32), vmem((groups, fronts) + tile, f32),
            vmem((groups, fronts) + tile, f32), vmem((groups, fronts) + tile, f32),
            vmem((fronts,) + tile, f32),
            vmem((fronts,) + tile, jnp.int32), vmem((fronts,) + tile, jnp.int32),
            vmem((groups, 2 * root_rb) + tile, f32),
            vmem((rows, groups, blks, root_rb) + tile, f32), vmem((sums, groups, root_blocks) + tile, f32),
            vmem((sums, groups, half, root_per) + tile, f32), vmem((casts, groups, root_blocks) + tile, f32),
            vmem((CHILD_ROWS, groups, blks, child_rb) + tile, f32),
            vmem((CHILD_SUMS, groups, child_blocks) + tile, f32),
            vmem((CHILD_SUMS, groups, half, child_per) + tile, f32),
            vmem((CHILD_SUMS, groups, child_blocks) + tile, f32),
            vmem((fronts, root_per) + tile, f32),
            pltpu.SMEM((sends,), jnp.int32), pltpu.SMEM((sends,), jnp.int32),
            pltpu.SMEM((fronts,), jnp.int32),
            sem((4 + root.shape[0],)),
            sem((rows + CHILD_ROWS, groups)), sem((rows + CHILD_ROWS, groups)),
            sem((sums + CHILD_SUMS, groups)), sem((sums + CHILD_SUMS, groups)),
            sem((casts + CHILD_SUMS, groups)), sem((casts + CHILD_SUMS, groups)),
            sem((2, groups)), sem((2, groups)), sem((1,)), sem((1,)),
        ],
        compiler_params=pltpu.CompilerParams(
            collective_id=0, has_side_effects=True, vmem_limit_bytes=58 * 1024 * 1024
        ),
    )(extend_map, rside, cside, root, child, child_update)
    return (outs[0][None], outs[1][None])


def solution(mesh):
    in_specs = (
        P("front", None, None, "blk"),
        P("front", None, None, "blk"),
        P("front", None, "blk"),
        P("front"),
        P("front", None, None, None),
        P("front", None, None, None),
    )
    out_specs = (P("front", None, None, None), P("front", None, None, None))
    body = functools.partial(on_device, mesh.shape["front"], mesh.shape["blk"])
    return jax.shard_map(body, mesh=mesh, in_specs=in_specs, out_specs=out_specs, check_vma=False)
```

time: 1650 us -> 194 us (0.12)
  waiting for transfers between devices: 1300 us -> 0 us
  Pallas kernels: 0 us -> 190 us
  blocking collectives: 119 us -> 0 us
  matrix products: 116 us -> 0 us
  other arithmetic: 53.3 us -> 0 us
  starting transfers between devices: 23.6 us -> 0 us
    psum x12 -> x0, waiting for transfers between devices: 1280 us -> none  [across_front(): return lax.psum(stacked, 'front')]
    pallas_call x0 -> x1, Pallas kernels: none -> 190 us  [on_device(): pl.pallas_call(functools.partial(kernel, fronts, blks), out_shape=(jax.Sh...]
    all_gather x12 -> x0, blocking collectives: 119 us -> none  [across_blk(): pieces = lax.all_gather(partial_rows, 'blk', axis=0, tiled=True)]
    dot_general x40 -> x0, matrix products: 116 us -> none  [the longest x24 69.7 us: times_tile(): return jnp.dot(vector, tile.astype(jnp.float32), precision=exact_mode)]
    another operation x35 -> x0, other arithmetic: 35.6 us -> none
    all_to_all x3 -> x0, starting transfers between devices: 23.1 us -> none  [the longest x1 9.6 us: on_device(): lax.all_to_all(slot_tags.reshape(fronts, capacity), 'front', split_axis=0...]
    all_to_all x3 -> x0, waiting for transfers between devices: 19.7 us -> none  [the longest x1 10.2 us: on_device(): lax.all_to_all(returning, 'front', split_axis=0, concat_axis=0, tiled=True)]
  transfers between devices with their start and end apart: 15 -> 0, of which waited for: 14 -> 0; matrix products, arithmetic and copies ran while one was open for 2% -> 0% of each run, Pallas kernels for 0% -> 0%
where the time goes in v2:
time: 194 us
  Pallas kernels  190 us (98%)
  local copies, waits for them, and re-layouts  2.98 us (2%)
    pallas_call x1, Pallas kernels, on_device(): pl.pallas_call(functools.partial(kernel, fronts, blks), out_shape=(jax.Sh...  190 us

profile of v2, /device:TPU:1, one launch (start us, length us, event | category | flops | bytes accessed | tf_op | source)
XLA Modules:
  0.0 193.6 jit_solution(8570773883777515752)
XLA Ops:
  0.6 190.0 %shard_map.77 = (f32[2,24,640]{2,1,0:T(8,128)}, f32[2,24,256]{2,1,0:T(8,128)}) custom-call(s32[12]{0:T(128)} %emap.1, f32[2,24,640]{2,1,0:T(8,128)} %bitcast.8, f32[2,24,256]{2,1,0:T(8,128)} %bitcast.10, bf16[5,640,2560]{2,1,0:T(8,128)(2,1)} %bitcast.6, bf16[3,256,1024]{2,1,0:T(8,128)(2,1)} %bitcast.7, bf16[1536,2,1024]{2,1,0:T(2,128)(2,1)} %gt_hbm.1), custom_call_target="tpu_custom_call" | custom-call | tf_op jit(solution)/shard_map/pallas_call | solution.py:550
  190.6 1.6 copy.10
  192.2 1.4 copy.11

commit v3 on v2

--- a/solution.py
+++ b/solution.py
@@ -66,13 +66,13 @@
     rt, ct, gv, gt, shuffle, run, xr, xv, xc, xvc, xn, pb, ob, ar, rk, ak, nk, tgs, tgr, zb,
     rows_r, term_r, recv_r, y_r, rows_c, term_c, recv_c, y_c,
     counts, own, place, inv,
-    load_sem, blk_s, blk_r, rs_s, rs_r, ag_s, ag_r, x_s, x_r, t_s, t_r,
+    load_sem, blk_s, blk_r, rs_s, rs_r, ag_s, ag_r, x_s, x_r, t_s, t_r, free,
 ):
     f = lax.axis_index("front")
     b = lax.axis_index("blk")
     half = fronts // 2
-    p = f // half
-    q = f % half
+    p = lax.div(f, half)
+    q = lax.rem(f, half)
     count_groups = rside.shape[1] // SUB
     root_rb = rside.shape[2] // LANES
     child_rb = cside.shape[2] // LANES
@@ -93,9 +93,9 @@
 
     barrier = pltpu.get_barrier_semaphore()
     loop(fronts, lambda i: pl.semaphore_signal(
-        barrier, inc=1, device_id=((f + i) % fronts, b), device_id_type=MESH), 1)
+        barrier, inc=1, device_id=(lax.rem(f + i, fronts), b), device_id_type=MESH), 1)
     loop(blks, lambda i: pl.semaphore_signal(
-        barrier, inc=1, device_id=(f, (b + i) % blks), device_id_type=MESH), 1)
+        barrier, inc=1, device_id=(f, lax.rem(b + i, blks)), device_id_type=MESH), 1)
 
     def remote(src, dst, ss, rs, device):
         pltpu.make_async_remote_copy(
@@ -111,10 +111,10 @@
         x=xc, v=xvc)
 
     def member_of(ch, g):
-        return (ch + 5 * g) % half
+        return lax.rem(ch + 5 * g, half)
 
     def chunk_of(member, g):
-        return (member + half - 5 * g % half) % half
+        return lax.rem(member + 4 * half - 5 * g, half)
 
     def at_pair(side, phase, table):
         return p if side is child else table[phase]
@@ -133,7 +133,7 @@
         ref = side.rows.at[phase, g, b]
         sems = (blk_s.at[side.blk0 + phase, g], blk_r.at[side.blk0 + phase, g])
         for d in range(1, blks):
-            remote(ref, ref, *sems, (f, (b + d) % blks))
+            remote(ref, ref, *sems, (f, lax.rem(b + d, blks)))
 
     def rows_out(side, phase, g, tile, slot, base=None):
         product = fold(times_transposed(x_group(side.v, g)[...], tile[slot]))
@@ -207,7 +207,7 @@
         target = p if side is child else CAST_TO[phase][0]
 
         def send(i):
-            remote(ref, ref, *sems, (target * half + (q + i) % half, b))
+            remote(ref, ref, *sems, (target * half + lax.rem(q + i, half), b))
         loop(half, send, 1 if side is child or target == source else 0)
 
     def spread_more(phase, g):
@@ -217,7 +217,7 @@
             target = CAST_TO[phase][1]
 
             def send(i):
-                remote(ref, ref, ag_s.at[phase, g], ag_r.at[phase, g], (target * half + (q + i) % half, b))
+                remote(ref, ref, ag_s.at[phase, g], ag_r.at[phase, g], (target * half + lax.rem(q + i, half), b))
             loop(half, send, 1 if target == CAST_FROM[phase] else 0)
 
     def gather(side, phase, g):
@@ -291,7 +291,7 @@
     tgr[f] = tgs[f]
 
     def send_tag(i):
-        u = (f + i) % fronts
+        u = lax.rem(f + i, fronts)
         remote(tgs.at[u], tgr.at[f], t_s.at[0], t_r.at[0], (u, b))
     loop(fronts, send_tag, 1)
     load_g.wait()
@@ -330,7 +330,7 @@
         ar[g, f] = pb[g, inv[f]]
 
         def send_block(i):
-            u = (f + i) % fronts
+            u = lax.rem(f + i, fronts)
             ob[g, u] = pb[g, inv[u]]
             remote(ob.at[g, u], ar.at[g, f], x_s.at[0, g], x_r.at[0, g], (u, b))
         loop(fronts, send_block, 1)
@@ -401,7 +401,7 @@
             return block
 
         def send_answer(i):
-            u = (f + i) % fronts
+            u = lax.rem(f + i, fronts)
             rk[g, u] = answer(u)
             remote(rk.at[g, u], ak.at[g, f], x_s.at[1, g], x_r.at[1, g], (u, b))
         loop(fronts, send_answer, 1)
@@ -417,10 +417,14 @@
             send_rows(root, 0, g)
     groups(first)
 
+    def links_free(index):
+        pl.semaphore_signal(free.at[index], inc=1, device_id=(f - half, b), device_id_type=MESH)
+
     @functools.partial(on, 0)
     def _():
         solve(0, 0)
         groups(lambda g: step(root, 0, 0, g))
+        pl.semaphore_wait(free.at[0], 1)
         groups(lambda g: spread_more(0, g))
         groups(lambda g: gather(root, 0, g))
         subtract(1)
@@ -432,8 +436,9 @@
         retreat(3, 4, 1, 4)
         finish(4, 1, lambda g: cols_out(root, BACK_2, g, xr, rt, 3))
         cols_whole(root, EARLY_1, xr, rt, 2)
+        cols_whole(root, EARLY_0, xr, rt, 1)
+        pl.semaphore_wait(free.at[1], 1)
         groups(lambda g: send_chunks(root, EARLY_1, g))
-        cols_whole(root, EARLY_0, xr, rt, 1)
         groups(lambda g: send_chunks(root, EARLY_0, g))
         groups(lambda g: step(root, BACK_0, 6, g, base=0, early=EARLY_0))
         retreat(6, 7, 0, 0)
@@ -442,6 +447,7 @@
     @functools.partial(on, 1)
     def _():
         advance(0, 1, 0, 0)
+        links_free(0)
         subtract(2)
         solve(1, 1)
         groups(lambda g: step(root, 1, 1, g))
@@ -451,12 +457,53 @@
         groups(lambda g: step(root, 2, 2, g))
         groups(lambda g: step(root, BACK_2, 4, g, base=2))
         retreat(4, 5, 1, 4)
+        links_free(1)
         finish(5, 1, lambda g: cols_out(root, BACK_1, g, xr, rt, 3))
         cols_whole(root, BACK_0, xr, rt, 2)
         groups(lambda g: step(root, BACK_1, 5, g, base=1, early=EARLY_1))
         retreat(5, 6, 0, 1)
         finish(6, 0, lambda g: cols_out(root, BACK_0, g, xr, rt, 0, add=True))
         groups(lambda g: answers(g))
+
+    def drain_terms(side, phase, g, same):
+        def some(count):
+            wait_bytes(side.term.at[phase, g, pl.ds(0, side.per * count)], rs_s.at[side.rs0 + phase, g])
+        if same:
+            both(mine(side, at_pair(side, phase, SUM_AT), g), lambda: some(side.chunks - 1), lambda: some(side.chunks))
+        else:
+            some(side.chunks)
+
+    def drain_rows(side, phase, g):
+        wait_bytes(side.rows.at[phase, g, pl.ds(0, blks - 1)], blk_s.at[side.blk0 + phase, g])
+
+    def drain_root(g):
+        for pair in range(2):
+            @functools.partial(on, pair)
+            def _(pair=pair):
+                for phase, source in enumerate(SUM_FROM):
+                    if source == pair:
+                        drain_terms(root, phase, g, SUM_AT[phase] == pair)
+                for phase, source in enumerate(ROOT_ROWS):
+                    if source == pair:
+                        drain_rows(root, phase, g)
+
+                @pl.when(mine(root, pair, g))
+                def _():
+                    for phase, source in enumerate(CAST_FROM):
+                        if source == pair:
+                            count = half * len(CAST_TO[phase]) - (source in CAST_TO[phase])
+                            wait_bytes(counts.at[pl.ds(0, count)], ag_s.at[phase, g])
+
+    def drain_child(g, sums, rows):
+        for phase in sums:
+            drain_terms(child, phase, g, True)
+        for phase in rows:
+            drain_rows(child, phase, g)
+
+        @pl.when(mine(child, None, g))
+        def _():
+            for phase in sums:
+                wait_bytes(recv_c.at[phase, g, pl.ds(0, half - 1)], ag_s.at[child.ag0 + phase, g])
 
     def child_3(g):
         wait_bytes(ak.at[g, pl.ds(0, fronts - 1)], x_r.at[1, g])
@@ -469,6 +516,7 @@
         cols_out(child, 2, g, xn, gt, 1)
     groups(child_3)
     cols_whole(child, 3, xn, gt, 0)
+    groups(drain_root)
     groups(lambda g: step(child, 2, 2, g, base=1))
 
     def child_4(g):
@@ -485,7 +533,15 @@
         rows_in(child, 1, g, last(1, g))
         cols_out(child, 3, g, xc, ct, 1, add=True)
     groups(child_5)
+
+    def drain_early(g):
+        drain_child(g, (0, 1), (0, 1))
+        wait_bytes(ob.at[g, pl.ds(0, fronts - 1)], x_s.at[0, g])
+        wait_bytes(rk.at[g, pl.ds(0, fronts - 1)], x_s.at[1, g])
+    groups(drain_early)
+    wait_bytes(tgs.at[pl.ds(0, fronts - 1)], t_s.at[0])
     groups(lambda g: step(child, 3, 3, g, base=0))
+    groups(lambda g: drain_child(g, (2,), ()))
 
     def child_6(g):
         gather(child, 3, g)
@@ -493,39 +549,11 @@
     groups(child_6)
     groups(lambda g: rows_in(child, 2, g, last(0, g)))
 
-    def drain(g):
-        def sent_chunks(side, phase, count):
-            wait_bytes(side.term.at[phase, g, pl.ds(0, side.per * count)], rs_s.at[side.rs0 + phase, g])
-
-        def sent_terms(side, phase, same):
-            if same:
-                both(mine(side, at_pair(side, phase, SUM_AT), g),
-                     lambda: sent_chunks(side, phase, side.chunks - 1),
-                     lambda: sent_chunks(side, phase, side.chunks))
-            else:
-                sent_chunks(side, phase, side.chunks)
-        for phase in range(len(SUM_FROM)):
-            on(SUM_FROM[phase], lambda phase=phase: sent_terms(root, phase, SUM_FROM[phase] == SUM_AT[phase]))
-        for phase in range(CHILD_SUMS):
-            sent_terms(child, phase, True)
-        for phase, pair in enumerate(ROOT_ROWS):
-            on(pair, lambda phase=phase: wait_bytes(rows_r.at[phase, g, pl.ds(0, blks - 1)], blk_s.at[phase, g]))
-        for phase in range(CHILD_ROWS):
-            wait_bytes(rows_c.at[phase, g, pl.ds(0, blks - 1)], blk_s.at[child.blk0 + phase, g])
-        for phase, source in enumerate(CAST_FROM):
-            @pl.when(mine(root, source, g))
-            def _(phase=phase, source=source):
-                count = half * len(CAST_TO[phase]) - (source in CAST_TO[phase])
-                wait_bytes(counts.at[pl.ds(0, count)], ag_s.at[phase, g])
-
-        @pl.when(mine(child, None, g))
-        def _():
-            for phase in range(CHILD_SUMS):
-                wait_bytes(recv_c.at[phase, g, pl.ds(0, half - 1)], ag_s.at[child.ag0 + phase, g])
-        wait_bytes(ob.at[g, pl.ds(0, fronts - 1)], x_s.at[0, g])
-        wait_bytes(rk.at[g, pl.ds(0, fronts - 1)], x_s.at[1, g])
-    groups(drain)
-    wait_bytes(tgs.at[pl.ds(0, fronts - 1)], t_s.at[0])
+    groups(lambda g: drain_child(g, (3,), (2,)))
+
+def place_fields(root_in, child_in, root_out, child_out):
+    root_out[0] = root_in[...]
+    child_out[0] = child_in[...]
 
 
 def on_device(fronts, blks, root_tiles, child_tiles, child_update, extend_map, root_side, child_side):
@@ -579,12 +607,18 @@
             sem((sums + CHILD_SUMS, groups)), sem((sums + CHILD_SUMS, groups)),
             sem((casts + CHILD_SUMS, groups)), sem((casts + CHILD_SUMS, groups)),
             sem((2, groups)), sem((2, groups)), sem((1,)), sem((1,)),
+            pltpu.SemaphoreType.REGULAR((2,)),
         ],
         compiler_params=pltpu.CompilerParams(
             collective_id=0, has_side_effects=True, vmem_limit_bytes=58 * 1024 * 1024
         ),
     )(extend_map, rside, cside, root, child, child_update)
-    return (outs[0][None], outs[1][None])
+    outs = pl.pallas_call(
+        place_fields,
+        out_shape=tuple(jax.ShapeDtypeStruct((1,) + o.shape, f32) for o in outs),
+        in_specs=[whole, whole], out_specs=(whole, whole),
+    )(*outs)
+    return tuple(outs)
 
 
 def solution(mesh):

time: 194 us -> 190 us (0.979)
  local copies, waits for them, and re-layouts: 2.98 us -> 0 us
    unnamed x2 -> x0, local copies, waits for them, and re-layouts: 2.98 us -> none
    pallas_call x1, Pallas kernels: 190 us -> 188 us  [on_device(): pl.pallas_call(functools.partial(kernel, fronts, blks), out_shape=(jax.Sh...]
where the time goes in v3:
time: 190 us
  Pallas kernels  189 us (99%)
    pallas_call x1, Pallas kernels, on_device(): pl.pallas_call(functools.partial(kernel, fronts, blks), out_shape=(jax.Sh...  188 us

profile of v3, /device:TPU:1, one launch (start us, length us, event | category | flops | bytes accessed | tf_op | source)
XLA Modules:
  0.0 190.0 jit_solution(8509569751051914314)
XLA Ops:
  0.6 187.7 %shard_map.77 = (f32[2,24,640]{2,1,0:T(8,128)}, f32[2,24,256]{2,1,0:T(8,128)}) custom-call(s32[12]{0:T(128)} %emap.1, f32[2,24,640]{2,1,0:T(8,128)} %bitcast.6, f32[2,24,256]{2,1,0:T(8,128)} %bitcast.7, bf16[5,640,2560]{2,1,0:T(8,128)(2,1)} %bitcast.4, bf16[3,256,1024]{2,1,0:T(8,128)(2,1)} %bitcast.5, bf16[1536,2,1024]{2,1,0:T(2,128)(2,1)} %gt_hbm.1), custom_call_target="tpu_custom_call" | custom-call | tf_op jit(solution)/shard_map/pallas_call | solution.py:578
  188.4 1.6 shard_map.78

commit v4 on v3

--- a/solution.py
+++ b/solution.py
@@ -15,9 +15,10 @@
 
 BACK_2, BACK_1, BACK_0, EARLY_1, EARLY_0 = 4, 5, 6, 7, 8
 SUM_FROM = (0, 1, 1, 0, 0, 1, 1, 0, 0)
-SUM_AT = (0, 1, 1, 0, 1, 1, 0, 1, 0)
-CAST_FROM = (0, 1, 1, 0, 1, 1, 0)
-CAST_TO = ((1, 0), (1, 0), (0,), (0,), (1,), (1,), (0,))
+SUM_AT = (0, 1, 1, 0, 1, 1, 0, 0, 0)
+CAST_FROM = (0, 1, 1, 0, 1, 1, 0, 0)
+CAST_TO = ((1, 0), (1,), (0,), (0,), (1,), (1,), (0,), (0,))
+AGAIN_1 = 7
 ROOT_ROWS = (0, 1, 1, 0, 0, 1, 1, 0)
 CHILD_SUMS, CHILD_ROWS = 4, 3
 
@@ -65,8 +66,8 @@
     emap, rside, cside, rt_hbm, ct_hbm, gt_hbm, rout, cout,
     rt, ct, gv, gt, shuffle, run, xr, xv, xc, xvc, xn, pb, ob, ar, rk, ak, nk, tgs, tgr, zb,
     rows_r, term_r, recv_r, y_r, rows_c, term_c, recv_c, y_c,
-    counts, own, place, inv,
-    load_sem, blk_s, blk_r, rs_s, rs_r, ag_s, ag_r, x_s, x_r, t_s, t_r, free,
+    counts, relay_in, relay_out, own, place, inv,
+    load_sem, blk_s, blk_r, rs_s, rs_r, ag_s, ag_r, x_s, x_r, t_s, t_r, relay_s, relay_r, free,
 ):
     f = lax.axis_index("front")
     b = lax.axis_index("blk")
@@ -233,7 +234,7 @@
         def _():
             total = take(side, phase, g)
             if early is not None:
-                total = total + take(side, early, g)
+                total = total + early(g)
             if base is not None:
                 total = side.y[base, g, pl.ds(side.per * chunk_of(q, g), side.per)] - total
             spread(side, out, g, total)
@@ -347,7 +348,7 @@
             tag = tgr[u]
             return tuple(t + jnp.where(tag == s, block, 0.0) for s, t in enumerate(totals))
         zero = jnp.zeros((SUB, LANES), jnp.float32)
-        landed = lax.fori_loop(0, fronts, add, (zero,) * (2 * root_rb), unroll=4)
+        landed = lax.fori_loop(0, fronts, add, (zero,) * (2 * root_rb), unroll=16)
         for h in range(2):
             for i in range(root_rb):
                 run[g, h, i] = lead * side_rows(rside, h, g, i) - landed[h * root_rb + i]
@@ -417,6 +418,29 @@
             send_rows(root, 0, g)
     groups(first)
 
+    def relay(index, g, value, peer):
+        relay_out[index, g] = value
+        remote(relay_out.at[index, g], relay_in.at[index, g], relay_s.at[index, g], relay_r.at[index, g], (peer, b))
+
+    def relayed(index, g):
+        wait_bytes(relay_in.at[index, g], relay_r.at[index, g])
+        return relay_in[index, g]
+
+    def relay_y(g):
+        @pl.when(mine(root, 1, g))
+        def _():
+            relay(0, g, root.y[1, g, pl.ds(root.per * chunk_of(q, g), root.per)], f - half)
+
+    def spread_y(g):
+        @pl.when(mine(root, 0, g))
+        def _():
+            spread(root, AGAIN_1, g, relayed(0, g))
+
+    def relay_sum(g):
+        @pl.when(mine(root, 0, g))
+        def _():
+            relay(1, g, take(root, EARLY_1, g), f + half)
+
     def links_free(index):
         pl.semaphore_signal(free.at[index], inc=1, device_id=(f - half, b), device_id_type=MESH)
 
@@ -428,7 +452,8 @@
         groups(lambda g: spread_more(0, g))
         groups(lambda g: gather(root, 0, g))
         subtract(1)
-        groups(lambda g: gather(root, 1, g))
+        groups(spread_y)
+        groups(lambda g: gather(root, AGAIN_1, g))
         subtract(2)
         advance(2, 3, 1, 3)
         solve(3, 4)
@@ -440,7 +465,8 @@
         pl.semaphore_wait(free.at[1], 1)
         groups(lambda g: send_chunks(root, EARLY_1, g))
         groups(lambda g: send_chunks(root, EARLY_0, g))
-        groups(lambda g: step(root, BACK_0, 6, g, base=0, early=EARLY_0))
+        groups(relay_sum)
+        groups(lambda g: step(root, BACK_0, 6, g, base=0, early=lambda g: take(root, EARLY_0, g)))
         retreat(6, 7, 0, 0)
         finish(7, 0, lambda g: answers(g))
 
@@ -452,15 +478,15 @@
         solve(1, 1)
         groups(lambda g: step(root, 1, 1, g))
         advance(1, 2, 1, 3)
-        groups(lambda g: spread_more(1, g))
+        groups(relay_y)
         solve(2, 4)
         groups(lambda g: step(root, 2, 2, g))
         groups(lambda g: step(root, BACK_2, 4, g, base=2))
+        links_free(1)
         retreat(4, 5, 1, 4)
-        links_free(1)
         finish(5, 1, lambda g: cols_out(root, BACK_1, g, xr, rt, 3))
         cols_whole(root, BACK_0, xr, rt, 2)
-        groups(lambda g: step(root, BACK_1, 5, g, base=1, early=EARLY_1))
+        groups(lambda g: step(root, BACK_1, 5, g, base=1, early=lambda g: relayed(1, g)))
         retreat(5, 6, 0, 1)
         finish(6, 0, lambda g: cols_out(root, BACK_0, g, xr, rt, 0, add=True))
         groups(lambda g: answers(g))
@@ -489,6 +515,7 @@
 
                 @pl.when(mine(root, pair, g))
                 def _():
+                    wait_bytes(relay_out.at[1 - pair, g], relay_s.at[1 - pair, g])
                     for phase, source in enumerate(CAST_FROM):
                         if source == pair:
                             count = half * len(CAST_TO[phase]) - (source in CAST_TO[phase])
@@ -600,6 +627,7 @@
             vmem((CHILD_SUMS, groups, half, child_per) + tile, f32),
             vmem((CHILD_SUMS, groups, child_blocks) + tile, f32),
             vmem((fronts, root_per) + tile, f32),
+            vmem((2, groups, root_per) + tile, f32), vmem((2, groups, root_per) + tile, f32),
             pltpu.SMEM((sends,), jnp.int32), pltpu.SMEM((sends,), jnp.int32),
             pltpu.SMEM((fronts,), jnp.int32),
             sem((4 + root.shape[0],)),
@@ -607,6 +635,7 @@
             sem((sums + CHILD_SUMS, groups)), sem((sums + CHILD_SUMS, groups)),
             sem((casts + CHILD_SUMS, groups)), sem((casts + CHILD_SUMS, groups)),
             sem((2, groups)), sem((2, groups)), sem((1,)), sem((1,)),
+            sem((2, groups)), sem((2, groups)),
             pltpu.SemaphoreType.REGULAR((2,)),
         ],
         compiler_params=pltpu.CompilerParams(

time: 190 us -> 187 us (0.984)
  Pallas kernels: 189 us -> 186 us
    pallas_call x1, Pallas kernels: 188 us -> 185 us  [on_device(): pl.pallas_call(functools.partial(kernel, fronts, blks), out_shape=(jax.Sh...]
where the time goes in v4:
time: 187 us
  Pallas kernels  186 us (99%)
    pallas_call x1, Pallas kernels, on_device(): pl.pallas_call(functools.partial(kernel, fronts, blks), out_shape=(jax.Sh...  185 us

profile of v4, /device:TPU:1, one launch (start us, length us, event | category | flops | bytes accessed | tf_op | source)
XLA Modules:
  0.0 186.8 jit_solution(16294914952628095263)
XLA Ops:
  0.6 184.6 %shard_map.77 = (f32[2,24,640]{2,1,0:T(8,128)}, f32[2,24,256]{2,1,0:T(8,128)}) custom-call(s32[12]{0:T(128)} %emap.1, f32[2,24,640]{2,1,0:T(8,128)} %bitcast.6, f32[2,24,256]{2,1,0:T(8,128)} %bitcast.7, bf16[5,640,2560]{2,1,0:T(8,128)(2,1)} %bitcast.4, bf16[3,256,1024]{2,1,0:T(8,128)(2,1)} %bitcast.5, bf16[1536,2,1024]{2,1,0:T(2,128)(2,1)} %gt_hbm.1), custom_call_target="tpu_custom_call" | custom-call | tf_op jit(solution)/shard_map/pallas_call | solution.py:605
  185.2 1.6 shard_map.78

commit v5 on v4

--- a/solution.py
+++ b/solution.py
@@ -441,8 +441,8 @@
         def _():
             relay(1, g, take(root, EARLY_1, g), f + half)
 
-    def links_free(index):
-        pl.semaphore_signal(free.at[index], inc=1, device_id=(f - half, b), device_id_type=MESH)
+    def links_free(index, peer):
+        pl.semaphore_signal(free.at[index], inc=1, device_id=(peer, b), device_id_type=MESH)
 
     @functools.partial(on, 0)
     def _():
@@ -467,13 +467,14 @@
         groups(lambda g: send_chunks(root, EARLY_0, g))
         groups(relay_sum)
         groups(lambda g: step(root, BACK_0, 6, g, base=0, early=lambda g: take(root, EARLY_0, g)))
+        links_free(2, f + half)
         retreat(6, 7, 0, 0)
         finish(7, 0, lambda g: answers(g))
 
     @functools.partial(on, 1)
     def _():
         advance(0, 1, 0, 0)
-        links_free(0)
+        links_free(0, f - half)
         subtract(2)
         solve(1, 1)
         groups(lambda g: step(root, 1, 1, g))
@@ -482,13 +483,14 @@
         solve(2, 4)
         groups(lambda g: step(root, 2, 2, g))
         groups(lambda g: step(root, BACK_2, 4, g, base=2))
-        links_free(1)
+        links_free(1, f - half)
         retreat(4, 5, 1, 4)
         finish(5, 1, lambda g: cols_out(root, BACK_1, g, xr, rt, 3))
         cols_whole(root, BACK_0, xr, rt, 2)
         groups(lambda g: step(root, BACK_1, 5, g, base=1, early=lambda g: relayed(1, g)))
         retreat(5, 6, 0, 1)
         finish(6, 0, lambda g: cols_out(root, BACK_0, g, xr, rt, 0, add=True))
+        pl.semaphore_wait(free.at[2], 1)
         groups(lambda g: answers(g))
 
     def drain_terms(side, phase, g, same):
@@ -636,7 +638,7 @@
             sem((casts + CHILD_SUMS, groups)), sem((casts + CHILD_SUMS, groups)),
             sem((2, groups)), sem((2, groups)), sem((1,)), sem((1,)),
             sem((2, groups)), sem((2, groups)),
-            pltpu.SemaphoreType.REGULAR((2,)),
+            pltpu.SemaphoreType.REGULAR((3,)),
         ],
         compiler_params=pltpu.CompilerParams(
             collective_id=0, has_side_effects=True, vmem_limit_bytes=58 * 1024 * 1024

time: 187 us -> 183 us (0.979)
  Pallas kernels: 186 us -> 181 us
    pallas_call x1, Pallas kernels: 185 us -> 180 us  [on_device(): pl.pallas_call(functools.partial(kernel, fronts, blks), out_shape=(jax.Sh...]
where the time goes in v5:
time: 183 us; the launch traced here: 182 us
  Pallas kernels  181 us (99%)
    pallas_call x1, Pallas kernels, on_device(): pl.pallas_call(functools.partial(kernel, fronts, blks), out_shape=(jax.Sh...  180 us

profile of v5, /device:TPU:1, one launch (start us, length us, event | category | flops | bytes accessed | tf_op | source)
XLA Modules:
  0.0 182.1 jit_solution(4742519681101653401)
XLA Ops:
  0.6 179.9 %shard_map.77 = (f32[2,24,640]{2,1,0:T(8,128)}, f32[2,24,256]{2,1,0:T(8,128)}) custom-call(s32[12]{0:T(128)} %emap.1, f32[2,24,640]{2,1,0:T(8,128)} %bitcast.6, f32[2,24,256]{2,1,0:T(8,128)} %bitcast.7, bf16[5,640,2560]{2,1,0:T(8,128)(2,1)} %bitcast.4, bf16[3,256,1024]{2,1,0:T(8,128)(2,1)} %bitcast.5, bf16[1536,2,1024]{2,1,0:T(2,128)(2,1)} %gt_hbm.1), custom_call_target="tpu_custom_call" | custom-call | tf_op jit(solution)/shard_map/pallas_call | solution.py:607
  180.5 1.6 shard_map.78
